TPU v7x, 32 devices: a whole 2x2x4 slice. The times are simulated.
32 devices in a mesh: plane: 4 (over y, x), wire: 4 (over z), tick: 2 (over core).
Axes of the slice: x: 2, y: 2, z: 4, core: 2. Of those that a mesh axis runs over, the one named last changes fastest.
Arguments:
- raw: bfloat16 [4096, 4096], P(('plane', 'wire'), 'tick'), may hold values from -6 to 6
- chan_mask: int32 [4096], P(('plane', 'wire')), may hold values 0 or 1
- kernel: bfloat16 [4, 21, 256], P('plane'), may hold values from -0.078125 to 0.078125
- geometry: bfloat16 [128, 32, 128], replicated, may hold values from -1 to 1
- roi_block: int32 [3264], P(('plane', 'wire', 'tick')), may hold values from 0 to 127, as said below
- roi_owner: int32 [3264], P(('plane', 'wire', 'tick')), may hold values from 0 to 15, as said below
Outputs:
- signal: bfloat16 [4096, 4096], P(('plane', 'wire'), 'tick')
- image: float32 [2048, 4096], P(('plane', 'wire'), 'tick')
Inputs may be any that keep to these rules, and one draw needn't show every extreme that they name: `roi_block`: the 102 ids of one device are distinct. `roi_owner`: owner o is the device of the same tick shard whose index over plane and wire together is o. A device names one owner in at most 25 slots; in every tick shard one owner is named in exactly 25 slots by every device of that shard.
All inputs are finite; a program needn't handle non-finite values. No bound on the sum of `chan_mask` on one device may be relied on, other than what follows from the above.
Results may differ from a plain program's by a relative error of at most 0.0029.
Values may be sent and summed in bfloat16 or wider, within the bound.
No kernel may reach another device: no remote copies, remote signals or barrier semaphores. Data moves between devices by JAX's collectives and lax.ppermute only.
A program may use at most 64 MiB of HBM per device.

v0:
```python
import functools

import jax
import jax.numpy as jnp
from jax import lax
from jax.experimental import pallas as pl
from jax.experimental.pallas import tpu as pltpu
from jax.sharding import PartitionSpec as P

TB = 128
CAP = 25
PAD = 16
TABLE = 8
STEPS = 4
MIB = 1024 * 1024


def vmem():
    return pl.BlockSpec(memory_space=pltpu.VMEM)


def smem():
    return pl.BlockSpec(memory_space=pltpu.SMEM)


GROUP = 8


def home(position, planes, owner_total):
    return (position % planes) * (owner_total // planes) + position // planes


def lane_numbers():
    return lax.broadcasted_iota(jnp.int32, (1, 128), 1)


def earlier_lanes():
    return (
        lax.broadcasted_iota(jnp.int32, (128, 128), 0)
        < lax.broadcasted_iota(jnp.int32, (128, 128), 1)
    ).astype(jnp.bfloat16)


def count_before(member, before):
    return jnp.dot(
        member.astype(jnp.float32).astype(jnp.bfloat16), before, preferred_element_type=jnp.float32
    )


def most_named(owners, owner_total):
    lanes = lane_numbers()
    counts = jnp.full(owners.shape, -1.0, jnp.float32)
    for owner in range(owner_total):
        named = jnp.sum((owners == owner).astype(jnp.float32), axis=1, keepdims=True)
        counts = jnp.where(lanes == owner, named, counts)
    top = jnp.max(counts, axis=1, keepdims=True)
    chosen = jnp.min(
        jnp.where(counts == top, lanes.astype(jnp.float32), 127.0), axis=1, keepdims=True
    )
    return counts, chosen


def prepare_kernel(
    planes,
    owner_total,
    share,
    tick_total,
    raw_hbm,
    mask_hbm,
    owner_hbm,
    block_hbm,
    mask_out,
    first_ref,
    last_ref,
    own_ref,
    out_ref,
    *rest,
):
    wires, ticks = raw_hbm.shape
    count = 1 if tick_total == 2 else 2
    sides = rest[:count]
    side_refs = rest[count : 2 * count]
    first_buf, last_buf, mask_ref, owner_ref, block_ref, sems = rest[2 * count :]
    tick = lax.axis_index("tick")
    me = lax.axis_index("wire") * planes + lax.axis_index("plane")
    if tick_total == 2:
        starts = [pl.multiple_of((1 - tick) * (ticks - TB), TB)]
    else:
        starts = [0, ticks - TB]
    moves = [(mask_hbm, mask_ref), (owner_hbm, owner_ref), (block_hbm, block_ref)]
    moves += [(raw_hbm.at[:, pl.ds(start, TB)], ref) for start, ref in zip(starts, side_refs)]
    moves += [(raw_hbm.at[pl.ds(0, PAD)], first_buf), (raw_hbm.at[pl.ds(wires - PAD, PAD)], last_buf)]
    copies = [
        pltpu.make_async_copy(source, target, sems.at[index])
        for index, (source, target) in enumerate(moves)
    ]
    for copy in copies:
        copy.start()
    for copy in copies[:3]:
        copy.wait()

    for part in range(wires // 128):
        row = mask_ref[part : part + 1].astype(jnp.float32)
        wide = jnp.transpose(jnp.broadcast_to(row, (128, 128)))
        mask_out[part * 128 : (part + 1) * 128] = wide.astype(jnp.bfloat16)

    lanes = lane_numbers()
    slot_count = owner_ref.shape[1]
    owner = owner_ref[...]
    wire_shards = owner_total // planes
    none = owner_total * 128
    own_ref[...] = jnp.where(lanes == 127, none + me, none)
    own_ref[:, 0:slot_count] = (
        (owner % wire_shards) * planes + owner // wire_shards
    ) * 128 + block_ref[...]
    own = own_ref[...]
    _, hot = most_named(own >> 7, owner_total)
    rows = lax.broadcasted_iota(jnp.int32, (owner_total, 128), 0)
    member = (own >> 7) == rows
    rank = count_before(member, earlier_lanes())
    place = jnp.where(rank < share, rows.astype(jnp.float32) * share + rank, -1.0)
    place = jnp.where(rows.astype(jnp.float32) == hot, -2.0, place)
    place = jnp.sum(jnp.where(member, place + 3.0, 0.0), axis=0, keepdims=True)

    column = jnp.transpose(jnp.broadcast_to(own.astype(jnp.float32), (128, 128)))
    column = column.astype(jnp.int32)
    here = ((column & 127) == lanes) & ((column >> 7) < owner_total)
    spread = jnp.transpose(jnp.broadcast_to(place, (128, 128)))
    placed = jnp.sum(jnp.where(here, spread, 0.0), axis=0, keepdims=True)
    trash = float(owner_total * share)
    facts = jnp.where(lanes == 2, me, 0)
    out_ref[...] = jnp.zeros_like(out_ref)
    out_ref[0:1, :] = jnp.where(placed >= 3.0, placed - 3.0, trash).astype(jnp.int32)
    out_ref[1:2, :] = jnp.where(lanes == 0, hot.astype(jnp.int32), facts)
    out_ref[2:3, :] = (placed == 1.0).astype(jnp.int32)

    for copy in copies[3:]:
        copy.wait()
    for side, ref in zip(sides, side_refs):
        side[...] = ref[...] * mask_out[...]
    for block in range(ticks // TB):
        at = slice(block * TB, (block + 1) * TB)
        first_ref[:, at] = first_buf[:, at] * mask_out[0:PAD]
        last_ref[:, at] = last_buf[:, at] * mask_out[wires - PAD : wires]


def prepare(raw, chan_mask, roi_owner, roi_block, planes, owner_total, share):
    wires, ticks = raw.shape
    tick_total = lax.axis_size("tick")
    sides = 1 if tick_total == 2 else 2
    side = jax.ShapeDtypeStruct((wires, TB), jnp.bfloat16)
    edge = jax.ShapeDtypeStruct((PAD, ticks), jnp.bfloat16)
    row = jax.ShapeDtypeStruct((1, 128), jnp.int32)
    table = jax.ShapeDtypeStruct((8, 128), jnp.int32)
    slot_count = roi_owner.shape[0]
    return pl.pallas_call(
        functools.partial(prepare_kernel, planes, owner_total, share, tick_total),
        out_shape=(side, edge, edge, row, table) + (side,) * sides,
        in_specs=[pl.BlockSpec(memory_space=pltpu.HBM)] * 4,
        out_specs=(vmem(),) * (5 + sides),
        scratch_shapes=[pltpu.VMEM((wires, TB), jnp.bfloat16)] * sides
        + [pltpu.VMEM((PAD, ticks), jnp.bfloat16)] * 2
        + [pltpu.VMEM((wires // 128, 128), jnp.int32)]
        + [pltpu.VMEM((1, slot_count), jnp.int32)] * 2
        + [pltpu.SemaphoreType.DMA((sides + 5,))],
        compiler_params=pltpu.CompilerParams(vmem_limit_bytes=60 * MIB),
        name="prepare",
    )(raw, chan_mask.reshape(wires // 128, 128), roi_owner[None], roi_block[None])


def receive_kernel(owner_total, planes, share, wire_blocks, tick_blocks, rows_ref, own_ref, out_ref):
    lanes = lane_numbers()
    lane_f = lanes.astype(jnp.float32)
    every = rows_ref[...]
    owners = every >> 7
    own = own_ref[...]
    me = jnp.sum(jnp.where(lanes == 127, own & 127, 0).astype(jnp.float32), axis=1, keepdims=True)

    counts, chosen = most_named(owners, owner_total)
    hot = jnp.max(chosen, axis=0, keepdims=True)
    agreed = hot == jnp.min(chosen, axis=0, keepdims=True)
    left = jnp.where(agreed & (lane_f == hot), 0.0, counts)
    fullest = jnp.max(jnp.max(left, axis=1, keepdims=True), axis=0, keepdims=True)
    start = agreed.astype(jnp.float32)
    trips = -start
    for step in range(-(-CAP // share)):
        trips = trips + (fullest > step * share).astype(jnp.float32)
    trips = jnp.maximum(trips, 0.0)
    hot = jnp.where(agreed, hot, -1.0)

    to_me = owners.astype(jnp.float32) == me
    before = earlier_lanes()
    rank = count_before(to_me, before)
    blocks = every & 127
    source = lax.broadcasted_iota(jnp.int32, (owner_total, 128), 0)
    line = home(source, planes, owner_total) * wire_blocks + blocks // tick_blocks
    line = line.astype(jnp.float32)
    tick = (blocks % tick_blocks).astype(jnp.float32)
    lines = jnp.zeros((1, 128), jnp.float32)
    ticks = jnp.full((1, 128), -1.0, jnp.float32)
    for slot in range(share):
        got = to_me & (rank == slot)
        here = lanes == source * share + slot
        for value, where in ((line, 0), (tick + 1.0, 1)):
            one = jnp.sum(jnp.where(got, value, 0.0), axis=1, keepdims=True)
            one = jnp.sum(jnp.where(here, one, 0.0), axis=0, keepdims=True)
            if where == 0:
                lines = lines + one
            else:
                ticks = ticks + one

    block_rows = lax.broadcasted_iota(jnp.int32, (tick_blocks, 128), 0).astype(jnp.float32)
    member = block_rows == ticks
    rank = count_before(member, before)
    total = jnp.sum(member.astype(jnp.float32), axis=1, keepdims=True)
    groups = jnp.zeros_like(total)
    for step in range(0, owner_total * share, GROUP):
        groups = groups + (total > step).astype(jnp.float32)
    lower = (
        lax.broadcasted_iota(jnp.int32, (tick_blocks, tick_blocks), 0)
        > lax.broadcasted_iota(jnp.int32, (tick_blocks, tick_blocks), 1)
    ).astype(jnp.bfloat16)
    base = jnp.dot(
        lower,
        jnp.broadcast_to(groups, (tick_blocks, 128)).astype(jnp.bfloat16),
        preferred_element_type=jnp.float32,
    )
    place = jnp.sum(jnp.where(member, base * GROUP + rank, 0.0), axis=0, keepdims=True)
    trash = float(group_total(owner_total, share, tick_blocks) * GROUP)
    place = jnp.where(ticks < 0.0, trash, place)
    inside = (base <= lane_f) & (lane_f < base + groups)
    group_tick = jnp.sum(jnp.where(inside, block_rows, 0.0), axis=0, keepdims=True)

    facts = jnp.where(lanes == 0, hot, 0.0)
    facts = jnp.where(lanes == 1, trips, facts)
    facts = jnp.where(lanes == 2, me, facts)
    facts = jnp.where(lanes == 3, start, facts)
    out_ref[...] = jnp.zeros_like(out_ref)
    out_ref[0:1, :] = place.astype(jnp.int32)
    out_ref[1:2, :] = facts.astype(jnp.int32)
    out_ref[2:3, :] = lines.astype(jnp.int32)
    out_ref[3:4, :] = group_tick.astype(jnp.int32)


def group_total(owner_total, share, tick_blocks):
    return (owner_total * share - tick_blocks) // GROUP + tick_blocks


def make_receive_plan(rows, packed, owner_total, planes, share, wire_blocks, tick_blocks):
    return pl.pallas_call(
        functools.partial(receive_kernel, owner_total, planes, share, wire_blocks, tick_blocks),
        out_shape=jax.ShapeDtypeStruct((8, 128), jnp.int32),
        in_specs=[vmem(), vmem()],
        out_specs=vmem(),
        compiler_params=pltpu.CompilerParams(vmem_limit_bytes=2 * MIB),
        name="receive_plan",
    )(rows, packed)


def agree(rounds):
    devices = lax.axis_size("tick")
    reach = 1
    while reach < devices:
        ring = [(i, (i + reach) % devices) for i in range(devices)]
        rounds = jnp.maximum(rounds, lax.ppermute(rounds, "tick", ring))
        reach *= 2
    return rounds


def band_kernel(taps_w, taps_ref, band_ref):
    row = lax.broadcasted_iota(jnp.int32, (TB, TB), 0)
    col = lax.broadcasted_iota(jnp.int32, (TB, TB), 1)
    pairs = (taps_w + 1) // 2
    band_ref[0, 0 : 3 * TB, TB : 2 * TB] = jnp.zeros((3 * TB, TB), jnp.bfloat16)
    band_ref[pairs - 1, 3 * TB : 6 * TB, 0:TB] = jnp.zeros((3 * TB, TB), jnp.bfloat16)
    taps = taps_ref[...].astype(jnp.float32)
    for tap in range(taps_w):
        spread = jnp.broadcast_to(taps[tap : tap + 1], (TB, 2 * TB))
        rolled = pltpu.roll(spread, TB, 1, stride=1, stride_axis=0)
        middle = rolled[:, :TB]
        outer = rolled[:, TB:]
        bands = (
            jnp.where(col < row, outer, 0.0).astype(jnp.bfloat16),
            middle.astype(jnp.bfloat16),
            jnp.where(col >= row, outer, 0.0).astype(jnp.bfloat16),
        )
        for first, second in ((0, 0), (1, 1), (1, 0), (0, 1)):
            if (tap - first + second) % 2:
                continue
            pair = (tap - first + second) // 2
            for piece in range(3):
                start = (first * 3 + piece) * TB
                band_ref[pair, start : start + TB, second * TB : (second + 1) * TB] = bands[piece]


def make_bands(taps):
    taps_w = taps.shape[0]
    return pl.pallas_call(
        functools.partial(band_kernel, taps_w),
        out_shape=jax.ShapeDtypeStruct(((taps_w + 1) // 2, 6 * TB, 2 * TB), jnp.bfloat16),
        in_specs=[vmem()],
        out_specs=vmem(),
        cost_estimate=pl.CostEstimate(flops=10**9, bytes_accessed=6 * MIB, transcendentals=0),
        compiler_params=pltpu.CompilerParams(vmem_limit_bytes=16 * MIB),
        name="bands",
    )(taps)


def spread_pair(wide_ref, lhs_view, line, pitch, blocks):
    for side in range(2):
        for piece in range(3):
            at = (side * 3 + piece) * TB
            lhs_view[:, at : at + TB] = wide_ref[
                pl.ds((line + side) * pitch + piece, blocks), :
            ].astype(jnp.bfloat16)


def write_lines(total, out_view, signal_ref, line, pairs, blocks):
    for pair in range(pairs):
        for side in range(2):
            out_view[pl.ds((2 * pair + side) * blocks, blocks), :] = total[
                pair * blocks : (pair + 1) * blocks, side * TB : (side + 1) * TB
            ]
    for block in range(blocks):
        signal_ref[line : line + 2 * pairs, block * TB : (block + 1) * TB] = out_view[
            pl.ds(block, 2 * pairs, stride=blocks), :
        ].astype(jnp.bfloat16)


def inner_kernel(
    chunks,
    raw_ref,
    mask_ref,
    left_ref,
    right_ref,
    band_ref,
    inner_ref,
    wide_ref,
    lhs_ref,
    out_ref,
):
    wires, ticks = raw_ref.shape
    blocks = ticks // TB
    pitch = wide_ref.shape[0] // wires
    reach = band_ref.shape[0]
    span = 2 * PAD
    groups = wires // span

    def fill(group, block):
        lines = slice(group * span, (group + 1) * span)
        if block == 0:
            inner = left_ref[lines]
        elif block == blocks + 1:
            inner = right_ref[lines]
        else:
            inner = raw_ref[lines, (block - 1) * TB : block * TB] * mask_ref[lines]
        wide_ref[pl.ds(group * span * pitch + block, span, stride=pitch), :] = inner.astype(
            jnp.float32
        )

    margin = reach - 1
    begin = PAD // 2
    state = {"group": 0, "pair": begin}

    def prepare(upto):
        todo = []
        while state["pair"] < upto:
            line = 2 * state["pair"] - margin
            while state["group"] < groups and line + 1 >= state["group"] * span:
                group = state["group"]
                for block in range(blocks + 2):
                    todo.append(lambda group=group, block=block: fill(group, block))
                state["group"] += 1
            todo.append(
                lambda line=line, pair=state["pair"]: spread_pair(
                    wide_ref, lhs_ref.at[pair - begin], line, pitch, blocks
                )
            )
            state["pair"] += 1
        return todo

    pair = begin
    for job in prepare(pair + chunks[0] + margin):
        job()
    for index, size in enumerate(chunks):
        todo = prepare(pair + size + chunks[index + 1] + margin) if index + 1 < len(chunks) else []
        each = -(-len(todo) // reach)
        total = jnp.zeros((size * blocks, 2 * TB), jnp.float32)
        for step in range(0, reach, STEPS):
            steps = range(step, min(step + STEPS, reach))
            rows = [
                lhs_ref[pair - begin + one : pair - begin + one + size].reshape(
                    size * blocks, 6 * TB
                )
                for one in steps
            ]
            bands = band_ref[steps[0] : steps[-1] + 1].reshape(len(steps) * 6 * TB, 2 * TB)
            total = total + jnp.dot(
                jnp.concatenate(rows, axis=1), bands, preferred_element_type=jnp.float32
            )
            for job in todo[step * each : (steps[-1] + 1) * each]:
                job()
        write_lines(total, out_ref.at[index % 2], inner_ref, 2 * (pair - begin), size, blocks)
        pair += size


def convolve_inner(raw, mask, left, right, bands):
    wires, ticks = raw.shape
    reach = bands.shape[0]
    blocks = ticks // TB
    pitch = -(-(blocks + 2) // 8) * 8
    pairs = (wires - 2 * PAD) // 2
    chunks = []
    while sum(chunks) < pairs:
        chunks.append(min(32 if chunks else 16, pairs - sum(chunks)))
    flops = 2 * blocks * pairs * reach * 6 * TB * 2 * TB
    return pl.pallas_call(
        functools.partial(inner_kernel, tuple(chunks)),
        out_shape=jax.ShapeDtypeStruct((wires - 2 * PAD, ticks), jnp.bfloat16),
        in_specs=[vmem()] * 5,
        out_specs=vmem(),
        scratch_shapes=[
            pltpu.VMEM((wires * pitch, TB), jnp.float32),
            pltpu.VMEM((pairs + reach - 1, blocks, 6 * TB), jnp.bfloat16),
            pltpu.VMEM((2, 2 * max(chunks) * blocks, TB), jnp.float32),
        ],
        cost_estimate=pl.CostEstimate(flops=flops, bytes_accessed=6 * MIB, transcendentals=0),
        compiler_params=pltpu.CompilerParams(vmem_limit_bytes=28 * MIB),
        name="inner",
    )(raw, mask, left, right, bands)


def edge_kernel(
    planes,
    plan_ref,
    own_ref,
    inner_ref,
    raw_ref,
    mask_ref,
    left_ref,
    right_ref,
    top_ref,
    bottom_ref,
    band_ref,
    geo_ref,
    signal_ref,
    partial_ref,
    wide_ref,
    lhs_ref,
    out_ref,
    turned_ref,
):
    wires, ticks = signal_ref.shape
    blocks = ticks // TB
    reach = band_ref.shape[0]
    block_wires = geo_ref.shape[1]
    wire_blocks = wires // block_wires
    near = 2 * PAD
    lines = PAD + near
    pitch = wide_ref.shape[1] // lines
    pairs = PAD // 2
    margin = reach - 1

    signal_ref[PAD : wires - PAD] = inner_ref[...]
    source = home(plan_ref[1, 2], planes, geo_ref.shape[0] // wire_blocks)
    rows = geo_ref[pl.ds(source * wire_blocks, wire_blocks)].reshape(wires, -1)
    turned_ref[...] = jnp.transpose(rows)

    for end in range(2):
        halo_ref = (top_ref, bottom_ref)[end]
        mine = (slice(0, near), slice(wires - near, wires))[end]
        halo_at = (0, near)[end]
        mine_at = (PAD, 0)[end]
        for block in range(blocks + 2):
            columns = slice(block * TB, (block + 1) * TB)
            if block == 0:
                inner = left_ref[mine].astype(jnp.float32)
            elif block == blocks + 1:
                inner = right_ref[mine].astype(jnp.float32)
            else:
                inner = raw_ref[mine, (block - 1) * TB : block * TB] * mask_ref[mine]
                inner = inner.astype(jnp.float32)
            wide_ref[end, pl.ds(halo_at * pitch + block, PAD, stride=pitch), :] = halo_ref[
                :, columns
            ].astype(jnp.float32)
            wide_ref[end, pl.ds(mine_at * pitch + block, near, stride=pitch), :] = inner
        first = (PAD, near - PAD)[end] - margin
        for pair in range(pairs + margin):
            spread_pair(
                wide_ref.at[end], lhs_ref.at[end, pair], first + 2 * pair, pitch, blocks
            )

    total = jnp.zeros((2 * pairs * blocks, 2 * TB), jnp.float32)
    for step in range(0, reach, STEPS):
        steps = range(step, min(step + STEPS, reach))
        rows = jnp.concatenate(
            [
                jnp.concatenate(
                    [
                        lhs_ref[end, one : one + pairs].reshape(pairs * blocks, 6 * TB)
                        for one in steps
                    ],
                    axis=1,
                )
                for end in range(2)
            ],
            axis=0,
        )
        bands = band_ref[steps[0] : steps[-1] + 1].reshape(len(steps) * 6 * TB, 2 * TB)
        total = total + jnp.dot(rows, bands, preferred_element_type=jnp.float32)
    for end in range(2):
        write_lines(
            total[end * pairs * blocks : (end + 1) * pairs * blocks],
            out_ref.at[end],
            signal_ref,
            (0, wires - PAD)[end],
            pairs,
            blocks,
        )

    cells = geo_ref.shape[2]
    shards = partial_ref.shape[1] // cells
    own = own_ref[...]
    line = lax.broadcasted_iota(jnp.int32, (TABLE, 128), 0)
    table = jnp.where(line == 0, own >> 7, jnp.where(line == 1, own & 127, 0))
    table = table.astype(jnp.float32).astype(jnp.bfloat16)
    for plane in range(planes):
        partial_ref[plane, shards * cells : shards * cells + TABLE] = table

    for block in range(0, blocks, 2):
        chosen = []
        for side in range(2):
            at = slice((block + side) * TB, (block + side + 1) * TB)
            column = []
            for line in range(wire_blocks):
                tile = signal_ref[line * block_wires : (line + 1) * block_wires, at]
                asked = plan_ref[2, line * blocks + block + side] == 1
                column.append(jnp.where(asked, tile, jnp.zeros_like(tile)))
            chosen.append(jnp.concatenate(column, axis=0))
        sums = jnp.dot(
            turned_ref[...], jnp.concatenate(chosen, axis=1), preferred_element_type=jnp.float32
        ).astype(jnp.bfloat16)
        for side in range(2):
            shard, plane = divmod(block + side, planes)
            partial_ref[plane, shard * cells : (shard + 1) * cells] = sums[
                :, side * TB : (side + 1) * TB
            ]


def convolve_edges(
    planes, plan, own, inner, raw, mask, left, right, top, bottom, bands, geometry
):
    wires, ticks = raw.shape
    reach = bands.shape[0]
    cells = geometry.shape[2]
    blocks = ticks // TB
    pitch = -(-(blocks + 2) // 8) * 8
    flops = 2 * blocks * PAD * reach * 6 * TB * 2 * TB
    return pl.pallas_call(
        functools.partial(edge_kernel, planes),
        out_shape=(
            jax.ShapeDtypeStruct((wires, ticks), jnp.bfloat16),
            jax.ShapeDtypeStruct((planes, blocks // planes * cells + TABLE, TB), jnp.bfloat16),
        ),
        in_specs=[smem()] + [vmem()] * 10,
        out_specs=(vmem(), vmem()),
        scratch_shapes=[
            pltpu.VMEM((2, 3 * PAD * pitch, TB), jnp.float32),
            pltpu.VMEM((2, PAD // 2 + reach - 1, blocks, 6 * TB), jnp.bfloat16),
            pltpu.VMEM((2, PAD * blocks, TB), jnp.float32),
            pltpu.VMEM((cells, wires), jnp.bfloat16),
        ],
        cost_estimate=pl.CostEstimate(flops=flops, bytes_accessed=6 * MIB, transcendentals=0),
        compiler_params=pltpu.CompilerParams(vmem_limit_bytes=24 * MIB),
        name="edges",
    )(plan, own, inner, raw, mask, left, right, top, bottom, bands, geometry)


def fold_kernel(pieces_ref, out_ref):
    planes, height, _ = pieces_ref.shape
    shards, lines, _ = out_ref.shape
    cells = lines - TABLE
    line = lax.broadcasted_iota(jnp.int32, (TABLE, 128), 0)
    table = jnp.zeros((TABLE, 128), jnp.float32)
    for plane in range(planes):
        tags = pieces_ref[plane, height - TABLE : height].astype(jnp.float32)
        table = jnp.where(line == 2 * plane, tags[0:1], table)
        table = jnp.where(line == 2 * plane + 1, tags[1:2], table)
    for shard in range(shards):
        total = pieces_ref[0, shard * cells : (shard + 1) * cells].astype(jnp.float32)
        for plane in range(1, planes):
            total = total + pieces_ref[plane, shard * cells : (shard + 1) * cells].astype(
                jnp.float32
            )
        out_ref[shard, 0:cells] = total.astype(jnp.bfloat16)
        out_ref[shard, cells:lines] = table.astype(jnp.bfloat16)


def fold(pieces, shards):
    cells = (pieces.shape[1] - TABLE) // shards
    return pl.pallas_call(
        fold_kernel,
        out_shape=jax.ShapeDtypeStruct((shards, cells + TABLE, TB), jnp.bfloat16),
        in_specs=[vmem()],
        out_specs=vmem(),
        compiler_params=pltpu.CompilerParams(vmem_limit_bytes=4 * MIB),
        name="fold",
    )(pieces)


def pack_kernel(slots, plan_ref, signal_ref, payload_ref, tiles_ref):
    block_wires = payload_ref.shape[1]
    wires, ticks = signal_ref.shape
    blocks = ticks // TB
    tiles_ref[...] = jnp.zeros_like(tiles_ref)
    for line in range(wires // block_wires):
        for block in range(blocks):
            place = plan_ref[0, line * blocks + block]
            tiles_ref[place] = signal_ref[
                line * block_wires : (line + 1) * block_wires, block * TB : (block + 1) * TB
            ]
    payload_ref[...] = tiles_ref[0:slots]


def pack_tiles(plan, signal, slots, block_wires):
    return pl.pallas_call(
        functools.partial(pack_kernel, slots),
        out_shape=jax.ShapeDtypeStruct((slots, block_wires, TB), jnp.bfloat16),
        in_specs=[smem(), vmem()],
        out_specs=vmem(),
        scratch_shapes=[pltpu.VMEM((slots + 1, block_wires, TB), jnp.bfloat16)],
        cost_estimate=pl.CostEstimate(flops=10**8, bytes_accessed=3 * MIB, transcendentals=0),
        compiler_params=pltpu.CompilerParams(vmem_limit_bytes=8 * MIB),
        name="pack",
    )(plan, signal)


def stage_kernel(slots, plan_ref, geo_ref, out_ref, rows_ref):
    groups = out_ref.shape[0]
    rows_ref[...] = jnp.zeros_like(rows_ref)
    for slot in range(slots):
        rows_ref[plan_ref[0, slot]] = geo_ref[plan_ref[2, slot]]
    for group in range(groups):
        rows = rows_ref[group * GROUP : (group + 1) * GROUP]
        out_ref[group] = jnp.transpose(rows.reshape(-1, rows.shape[-1]))


def stage_geometry(plan, geometry, groups, slots):
    _, block_wires, cells = geometry.shape
    return pl.pallas_call(
        functools.partial(stage_kernel, slots),
        out_shape=jax.ShapeDtypeStruct((groups, cells, GROUP * block_wires), jnp.bfloat16),
        in_specs=[smem(), vmem()],
        out_specs=vmem(),
        scratch_shapes=[pltpu.VMEM((groups * GROUP + 1, block_wires, cells), jnp.bfloat16)],
        cost_estimate=pl.CostEstimate(flops=10**8, bytes_accessed=3 * MIB, transcendentals=0),
        compiler_params=pltpu.CompilerParams(vmem_limit_bytes=12 * MIB),
        name="stage",
    )(plan, geometry)


def image_kernel(owner_total, share, plan_ref, arrived_ref, staged_ref, image_ref, tiles_ref):
    cells, ticks = image_ref.shape
    block_wires = arrived_ref.shape[1]
    groups = staged_ref.shape[0]
    is_hot = plan_ref[1, 0] == plan_ref[1, 2]
    counts = plan_ref[1, 3] == 1

    @pl.when(is_hot)
    def _():
        for source in range(owner_total):
            sums = arrived_ref[source * share : source * share + cells // block_wires]
            image_ref[:, source * TB : (source + 1) * TB] = sums.reshape(cells, TB).astype(
                jnp.float32
            )

    @pl.when(jnp.logical_not(is_hot))
    def _():
        image_ref[...] = jnp.zeros_like(image_ref)
        tiles_ref[...] = jnp.zeros_like(tiles_ref)

        @pl.when(counts)
        def _():
            for slot in range(owner_total * share):
                tiles_ref[plan_ref[0, slot]] = arrived_ref[slot]
            for group in range(groups):
                tiles = tiles_ref[group * GROUP : (group + 1) * GROUP]
                at = pl.ds(pl.multiple_of(plan_ref[3, group] * TB, TB), TB)
                image_ref[:, at] += jnp.dot(
                    staged_ref[group],
                    tiles.reshape(GROUP * block_wires, TB),
                    preferred_element_type=jnp.float32,
                )


def make_image(plan, arrived, staged, owner_total, share, ticks):
    groups, cells, _ = staged.shape
    block_wires = arrived.shape[1]
    return pl.pallas_call(
        functools.partial(image_kernel, owner_total, share),
        out_shape=jax.ShapeDtypeStruct((cells, ticks), jnp.float32),
        in_specs=[smem(), vmem(), vmem()],
        out_specs=vmem(),
        scratch_shapes=[
            pltpu.VMEM((groups * GROUP + 1, block_wires, TB), jnp.bfloat16),
        ],
        cost_estimate=pl.CostEstimate(flops=10**8, bytes_accessed=3 * MIB, transcendentals=0),
        compiler_params=pltpu.CompilerParams(vmem_limit_bytes=16 * MIB),
        name="image",
    )(plan, arrived, staged)


def more_kernel(owner_total, planes, share, plan_ref, table_ref, arrived_ref, geo_ref, before_ref, image_ref):
    cells, ticks = image_ref.shape
    blocks = ticks // TB
    wire_blocks = geo_ref.shape[0] // owner_total
    image_ref[...] = before_ref[...]

    @pl.when(plan_ref[1, 0] != plan_ref[1, 2])
    def _():
        def add(source, carry):
            for slot in range(share):
                block = table_ref[source, slot]
                at = pl.multiple_of((block % blocks) * TB, TB)
                image_ref[:, pl.ds(at, TB)] += lax.dot_general(
                    geo_ref[home(source, planes, owner_total) * wire_blocks + block // blocks],
                    arrived_ref[source * share + slot],
                    (((0,), (0,)), ((), ())),
                    preferred_element_type=jnp.float32,
                )
            return carry

        lax.fori_loop(0, owner_total, add, 0)


def add_to_image(plan, table, arrived, geometry, owner_total, planes, share, image):
    return pl.pallas_call(
        functools.partial(more_kernel, owner_total, planes, share),
        out_shape=jax.ShapeDtypeStruct(image.shape, jnp.float32),
        in_specs=[smem(), smem()] + [vmem()] * 3,
        out_specs=vmem(),
        compiler_params=pltpu.CompilerParams(vmem_limit_bytes=16 * MIB),
        name="image_more",
    )(plan, table, arrived, geometry, image)


def further_round(
    trip, image, signal, geometry, rows, packed, plan, owner_total, planes, share
):
    trip, signal, rows, packed, plan = lax.optimization_barrier((trip, signal, rows, packed, plan))
    step = trip + plan[1, 3]
    hot = plan[1, 0]
    me = plan[1, 2]
    block_wires = geometry.shape[1]
    wire_count, tick_count = signal.shape
    blocks = tick_count // TB
    wire_blocks = wire_count // block_wires
    ids = jnp.arange(owner_total, dtype=jnp.int32)

    def ranks(owners):
        member = (owners[..., None] == ids).astype(jnp.int32)
        before = jnp.cumsum(member, axis=-2) - member
        return jnp.sum(before * member, axis=-1) - step * share

    def live(owners, rank):
        return (owners < owner_total) & (owners != hot) & (rank >= 0) & (rank < share)

    owners = packed[0] >> 7
    block = packed[0] & 127
    rank = ranks(owners)
    place = jnp.where(live(owners, rank), owners * share + rank, owner_total * share)
    tiles = signal.reshape(wire_blocks, block_wires, blocks, TB).transpose(0, 2, 1, 3)
    tiles = tiles.reshape(wire_blocks * blocks, block_wires, TB)[block]
    payload = jnp.zeros((owner_total * share, block_wires, TB), jnp.bfloat16)
    payload = payload.at[place].set(tiles, mode="drop")
    arrived = exchange(payload.reshape(owner_total, share, block_wires, TB))

    owners = rows >> 7
    rank = ranks(owners)
    source = jnp.arange(owner_total, dtype=jnp.int32)[:, None]
    line = jnp.where(live(owners, rank) & (owners == me), source, owner_total)
    table = jnp.zeros((owner_total, 128), jnp.int32)
    table = table.at[line, jnp.maximum(rank, 0)].set(rows & 127, mode="drop")
    return add_to_image(
        plan,
        table,
        arrived.reshape(owner_total * share, block_wires, TB),
        geometry,
        owner_total,
        planes,
        share,
        image,
    )


def tick_halo(sides):
    devices = lax.axis_size("tick")
    if devices == 2:
        tick = lax.axis_index("tick")
        got = lax.ppermute(sides[0], "tick", [(0, 1), (1, 0)])
        nothing = jnp.zeros_like(got)
        return jnp.where(tick == 0, nothing, got), jnp.where(tick == 0, got, nothing)
    up = [(i, i + 1) for i in range(devices - 1)]
    down = [(i + 1, i) for i in range(devices - 1)]
    return lax.ppermute(sides[1], "tick", up), lax.ppermute(sides[0], "tick", down)


def wire_halo(first, last, left, right):
    devices = lax.axis_size("wire")
    odd = lax.axis_index("wire") % 2 == 1
    last = jnp.concatenate([left[-PAD:], last, right[-PAD:]], axis=1)
    first = jnp.concatenate([left[:PAD], first, right[:PAD]], axis=1)
    got = []
    for begin, rows in ((0, jnp.where(odd, first, last)), (1, jnp.where(odd, last, first))):
        pairs = [(i, i + 1) for i in range(begin, devices - 1, 2)]
        got.append(lax.ppermute(rows, "wire", pairs + [(j, i) for i, j in pairs]))
    return jnp.where(odd, got[0], got[1]), jnp.where(odd, got[1], got[0])


def exchange(array, axes=("wire", "plane")):
    return lax.all_to_all(array, axes, split_axis=0, concat_axis=0, tiled=True)


def shards(raw, chan_mask, kernel, geometry, roi_block, roi_owner):
    wires, ticks = raw.shape
    slot_count = roi_block.shape[0]
    block_wires = geometry.shape[1]
    cells = geometry.shape[2]
    tick_blocks = ticks // TB
    planes = lax.axis_size("plane")
    wire_shards = lax.axis_size("wire")
    owner_total = planes * wire_shards
    share = -(-(slot_count - CAP) // (owner_total - 1))

    mask, first, last, packed, send_plan, *sides = prepare(
        raw, chan_mask, roi_owner, roi_block, planes, owner_total, share
    )
    left, right = tick_halo(sides)
    top, bottom = wire_halo(first, last, left, right)
    bands = make_bands(kernel[0])
    inner = convolve_inner(raw, mask, left, right, bands)
    signal, partial = convolve_edges(
        planes, send_plan, packed, inner, raw, mask, left, right, top, bottom, bands, geometry
    )

    pieces = exchange(partial, "plane")
    payload = pack_tiles(send_plan, signal, owner_total * share, block_wires)
    pieces, payload = lax.optimization_barrier((pieces, payload))
    pieces = exchange(fold(pieces, wire_shards), "wire")

    tables = pieces[:, cells : cells + 2 * planes].astype(jnp.int32)
    tables = tables.reshape(owner_total, 2, 128)
    rows = tables[:, 0] * 128 + tables[:, 1]
    plan = make_receive_plan(
        rows, packed, owner_total, planes, share, wires // block_wires, tick_blocks
    )
    staged = stage_geometry(
        plan, geometry, group_total(owner_total, share, tick_blocks), owner_total * share
    )

    sums = jnp.sum(pieces[:, :cells].astype(jnp.float32), axis=0).astype(jnp.bfloat16)
    payload = lax.dynamic_update_slice(
        payload.reshape(owner_total, share, block_wires, TB),
        sums.reshape(1, cells // block_wires, block_wires, TB),
        (send_plan[1, 0], 0, 0, 0),
    )
    arrived = exchange(payload).reshape(owner_total * share, block_wires, TB)
    image = make_image(plan, arrived, staged, owner_total, share, ticks)

    trips = agree(plan[1:2, 1:2])[0, 0]
    image = lax.fori_loop(
        0,
        trips,
        lambda trip, now: further_round(
            trip, now, signal, geometry, rows, packed, plan, owner_total, planes, share
        ),
        image,
    )
    return signal, image


def solution(mesh):
    in_specs = (
        P(("plane", "wire"), "tick"),
        P(("plane", "wire")),
        P("plane", None, None),
        P(),
        P(("plane", "wire", "tick")),
        P(("plane", "wire", "tick")),
    )
    out_specs = (P(("plane", "wire"), "tick"), P(("plane", "wire"), "tick"))
    return jax.shard_map(shards, mesh=mesh, in_specs=in_specs, out_specs=out_specs, check_vma=False)
```

profile of v0, /device:TPU:0, one launch (start us, length us, event | category | flops | bytes accessed | tf_op | source)
XLA Modules:
  0.0 70.0 jit_solution(7770672195408680191)
XLA Ops:
  0.6 1.9 %prepare.1 = (bf16[256,128]{1,0:T(8,128)(2,1)}, bf16[16,2048]{1,0:T(8,128)(2,1)}, bf16[16,2048]{1,0:T(8,128)(2,1)}, s32[1,128]{1,0:T(1,128)S(1)}, s32[8,128]{1,0:T(8,128)}, /*index=5*/bf16[256,128]{1,0:T(8,128)(2,1)}) custom-call(bf16[256,2048]{1,0:T(8,128)(2,1)} %raw_ref.3, s32[2,128]{1,0:T(2,128)} %bitcast.106, s32[1,102]{1,0:T(1,128)} %bitcast.107, ...), custom_call_target="tpu_custom_call" | custom-call | tf_op jit(solution)/shard_map/prepare/pallas_call | solution.py:156
  2.6 0.5 collective-permute-start
  3.1 0.7 %copy-done.3 = bf16[1,21,256]{2,1,0:T(8,128)(2,1)S(1)} copy-done((bf16[1,21,256]{2,1,0:T(8,128)(2,1)S(1)}, bf16[1,21,256]{2,1,0:T(8,128)(2,1)}, u32[]{:S(2)}) %copy-start.3) | copy-done | bytes 10776
  3.8 0.6 bands.1.band_ref
  4.5 0.2 copy-done.7
  4.7 2.7 %collective-permute-start.1 = (bf16[16,2304]{1,0:T(8,128)(2,1)S(1)}, bf16[16,2304]{1,0:T(8,128)(2,1)S(1)}, u32[]{:S(2)}, u32[]{:S(2)}) collective-permute-start(bf16[16,2304]{1,0:T(8,128)(2,1)S(1)} %get-tuple-element.129), channel_id=1, source_target_pairs={{0,2},{4,6},{2,0},{6,4},{1,3},{5,7},{3,1},{7,5},{8,10},{12,14},{10... | collective-permute-start | bytes 221192 | tf_op jit(solution)/shard_map/ppermute | solution.py:816
  7.4 0.7 collective-permute-start.2
  8.1 8.8 %inner.1.inner_ref = bf16[224,2048]{1,0:T(8,128)(2,1)S(1)} custom-call(bf16[256,2048]{1,0:T(8,128)(2,1)S(1)} %copy-done, bf16[256,128]{1,0:T(8,128)(2,1)S(1)} %copy-done.1, bf16[256,128]{1,0:T(8,128)(2,1)S(1)} %get-tuple-element.135.left_ref, bf16[256,128]{1,0:T(8,128)(2,1)S(1)} %get-tuple-element.134.right_ref, bf16[11,768,256]{2,1,0:T(8,128)(2,1)S(1)} %bands.1.band_ref), custom_call_target="tpu_custom_call" | custom-call | flops 7751073792 | bytes 6291456 | tf_op jit(solution)/shard_map/inner/pallas_call | solution.py:417
  16.9 3.4 %edges.1 = (bf16[256,2048]{1,0:T(8,128)(2,1)S(1)}, bf16[4,520,128]{2,1,0:T(8,128)(2,1)}) custom-call(s32[8,128]{1,0:T(8,128)S(1)} %copy-done.2, s32[1,128]{1,0:T(1,128)S(1)} %get-tuple-element.219.own_ref, bf16[224,2048]{1,0:T(8,128)(2,1)S(1)} %inner.1.inner_ref, bf16[256,2048]{1,0:T(8,128)(2,1)S(1)} %copy-done, bf16[256,128]{1,0:T(8,128)(2,1)S(1)} %copy-done.1, ...), custom_call_target="tpu_custom_call" | custom-call | flops 1107296256 | bytes 6291456 | tf_op jit(solution)/shard_map/edges/pallas_call | solution.py:559
  20.3 3.7 %all-to-all-start.1 = ((bf16[4,520,128]{2,1,0:T(8,128)(2,1)}), bf16[4,520,128]{2,1,0:T(8,128)(2,1)S(1)}, u32[]{:S(2)}, u32[]{:S(2)}) async-start(bf16[4,520,128]{2,1,0:T(8,128)(2,1)} %get-tuple-element.67), calls=%async_computation.1 | async-start | bytes 1064960 | tf_op jit(solution)/shard_map/all_to_all | solution.py:821
  24.0 1.8 %pack.1 = bf16[96,32,128]{2,1,0:T(8,128)(2,1)} custom-call(s32[8,128]{1,0:T(8,128)S(1)} %copy-done.2, bf16[256,2048]{1,0:T(8,128)(2,1)S(1)} %get-tuple-element.217.signal_ref), custom_call_target="tpu_custom_call" | custom-call | flops 100000000 | bytes 3145728 | tf_op jit(solution)/shard_map/pack/pallas_call | solution.py:626
  25.9 6.7 %all-to-all-done.1.pieces_ref = bf16[4,520,128]{2,1,0:T(8,128)(2,1)S(1)} async-done(((bf16[4,520,128]{2,1,0:T(8,128)(2,1)}), bf16[4,520,128]{2,1,0:T(8,128)(2,1)S(1)}, u32[]{:S(2)}, u32[]{:S(2)}) %all-to-all-start.1) | async-done | bytes 532512 | tf_op jit(solution)/shard_map/all_to_all | solution.py:821
  32.5 0.7 %fold.1 = bf16[4,136,128]{2,1,0:T(8,128)(2,1)} custom-call(bf16[4,520,128]{2,1,0:T(8,128)(2,1)S(1)} %all-to-all-done.1.pieces_ref), custom_call_target="tpu_custom_call" | custom-call | tf_op jit(solution)/shard_map/fold/pallas_call | solution.py:601
  33.2 5.5 %all-to-all-start.2 = ((bf16[4,136,128]{2,1,0:T(8,128)(2,1)}), bf16[4,136,128]{2,1,0:T(8,128)(2,1)S(1)}, u32[]{:S(2)}, u32[]{:S(2)}) async-start(bf16[4,136,128]{2,1,0:T(8,128)(2,1)} %fold.1), calls=%async_computation.2 | async-start | bytes 278528 | tf_op jit(solution)/shard_map/all_to_all | solution.py:821
  38.7 0.6 slice.47
  41.4 3.3 %all-to-all-done.2 = bf16[4,136,128]{2,1,0:T(8,128)(2,1)S(1)} async-done(((bf16[4,136,128]{2,1,0:T(8,128)(2,1)}), bf16[4,136,128]{2,1,0:T(8,128)(2,1)S(1)}, u32[]{:S(2)}, u32[]{:S(2)}) %all-to-all-start.2) | async-done | bytes 139296 | tf_op jit(solution)/shard_map/all_to_all | solution.py:821
  44.7 0.6 constant_dynamic-update-slice_fusion
  45.3 3.8 %all-to-all-start.3 = ((bf16[16,6,32,128]{3,2,1,0:T(8,128)(2,1)}), bf16[16,6,32,128]{3,2,1,0:T(8,128)(2,1)S(1)}, u32[]{:S(2)}, u32[]{:S(2)}) async-start(bf16[16,6,32,128]{3,2,1,0:T(8,128)(2,1)} %constant_dynamic-update-slice_fusion), calls=%async_computation.3 | async-start | bytes 1572864 | tf_op jit(solution)/shard_map/all_to_all | solution.py:821
  49.2 0.6 receive_plan.1.plan_ref
  49.8 0.7 %copy.39 = s32[16,128]{0,1:T(8,128)} copy(s32[16,128]{1,0:T(8,128)S(1)} %add_bitcast_fusion.rows_ref) | data formatting | bytes 16384 | tf_op jit(solution)/shard_map/while | solution.py:871
  50.5 0.6 slice.48
  51.1 1.4 %stage.1.staged_ref = bf16[26,128,256]{2,1,0:T(8,128)(2,1)S(1)} custom-call(s32[8,128]{1,0:T(8,128)S(1)} %receive_plan.1.plan_ref, bf16[128,32,128]{2,1,0:T(8,128)(2,1)S(1)} %copy-done.4), custom_call_target="tpu_custom_call" | custom-call | flops 100000000 | bytes 3145728 | tf_op jit(solution)/shard_map/stage/pallas_call | solution.py:650
  53.7 13.5 %all-to-all-done.3 = bf16[16,6,32,128]{3,2,1,0:T(8,128)(2,1)S(1)} async-done(((bf16[16,6,32,128]{3,2,1,0:T(8,128)(2,1)}), bf16[16,6,32,128]{3,2,1,0:T(8,128)(2,1)S(1)}, u32[]{:S(2)}, u32[]{:S(2)}) %all-to-all-start.3) | async-done | bytes 786464 | tf_op jit(solution)/shard_map/all_to_all | solution.py:821
  67.3 2.8 %image.1 = f32[128,2048]{1,0:T(8,128)} custom-call(s32[8,128]{1,0:T(8,128)S(1)} %receive_plan.1.plan_ref, bf16[96,32,128]{2,1,0:T(8,128)(2,1)S(1)} %bitcast.95, bf16[26,128,256]{2,1,0:T(8,128)(2,1)S(1)} %stage.1.staged_ref), custom_call_target="tpu_custom_call" | custom-call | flops 100000000 | bytes 3145728 | tf_op jit(solution)/shard_map/image/pallas_call | solution.py:699
  (33 shorter events, 0.2 us)
Async XLA Ops:
  0.6 7.4 %copy-start = (bf16[256,2048]{1,0:T(8,128)(2,1)S(1)}, bf16[256,2048]{1,0:T(8,128)(2,1)}, u32[]{:S(2)}) copy-start(bf16[256,2048]{1,0:T(8,128)(2,1)} %raw_ref.3) | copy-start | bytes 3145732
  2.6 5.5 %copy-start.1 = (bf16[256,128]{1,0:T(8,128)(2,1)S(1)}, bf16[256,128]{1,0:T(8,128)(2,1)}, u32[]{:S(2)}) copy-start(bf16[256,128]{1,0:T(8,128)(2,1)} %get-tuple-element.62.mask_ref) | copy-start | bytes 196612
  2.6 1.9 %collective-permute-start = (bf16[256,128]{1,0:T(8,128)(2,1)}, bf16[256,128]{1,0:T(8,128)(2,1)S(1)}, u32[]{:S(2)}, u32[]{:S(2)}) collective-permute-start(bf16[256,128]{1,0:T(8,128)(2,1)} %get-tuple-element.63), channel_id=1, source_target_pairs={{0,1},{1,0},{2,3},{3,2},{4,5},{5,4},{6,7},{7,6},{8,9},{9,8},{10,11... | collective-permute-start | bytes 196616 | tf_op jit(solution)/shard_map/ppermute | solution.py:800
  3.1 0.7 %copy-start.3 = (bf16[1,21,256]{2,1,0:T(8,128)(2,1)S(1)}, bf16[1,21,256]{2,1,0:T(8,128)(2,1)}, u32[]{:S(2)}) copy-start(bf16[1,21,256]{2,1,0:T(8,128)(2,1)} %param.10) | copy-start | bytes 32260
  3.8 0.8 %copy-start.7 = (bf16[16,2048]{1,0:T(8,128)(2,1)S(1)}, bf16[16,2048]{1,0:T(8,128)(2,1)}, u32[]{:S(2)}) copy-start(bf16[16,2048]{1,0:T(8,128)(2,1)} %get-tuple-element.64) | copy-start | bytes 196612
  3.8 0.9 %copy-start.8 = (bf16[16,2048]{1,0:T(8,128)(2,1)S(1)}, bf16[16,2048]{1,0:T(8,128)(2,1)}, u32[]{:S(2)}) copy-start(bf16[16,2048]{1,0:T(8,128)(2,1)} %get-tuple-element.65) | copy-start | bytes 196612
  4.7 12.1 %collective-permute-start.1 = (bf16[16,2304]{1,0:T(8,128)(2,1)S(1)}, bf16[16,2304]{1,0:T(8,128)(2,1)S(1)}, u32[]{:S(2)}, u32[]{:S(2)}) collective-permute-start(bf16[16,2304]{1,0:T(8,128)(2,1)S(1)} %get-tuple-element.129), channel_id=1, source_target_pairs={{0,2},{4,6},{2,0},{6,4},{1,3},{5,7},{3,1},{7,5},{8,10},{12,14},{10... | collective-permute-start | bytes 221192 | tf_op jit(solution)/shard_map/ppermute | solution.py:816
  7.4 9.5 %collective-permute-start.2 = (bf16[16,2304]{1,0:T(8,128)(2,1)S(1)}, bf16[16,2304]{1,0:T(8,128)(2,1)S(1)}, u32[]{:S(2)}, u32[]{:S(2)}) collective-permute-start(bf16[16,2304]{1,0:T(8,128)(2,1)S(1)} %get-tuple-element.128), channel_id=1, source_target_pairs={{2,4},{4,2},{3,5},{5,3},{10,12},{12,10},{11,13},{13,11},{18,20},{2... | collective-permute-start | bytes 221192 | tf_op jit(solution)/shard_map/ppermute | solution.py:816
  8.1 8.8 %copy-start.2 = (s32[8,128]{1,0:T(8,128)S(1)}, s32[8,128]{1,0:T(8,128)}, u32[]{:S(2)}) copy-start(s32[8,128]{1,0:T(8,128)} %get-tuple-element.60.plan_ref) | copy-start | bytes 12292
  8.1 8.8 %copy-start.4 = (bf16[128,32,128]{2,1,0:T(8,128)(2,1)S(1)}, bf16[128,32,128]{2,1,0:T(8,128)(2,1)}, u32[]{:S(2)}) copy-start(bf16[128,32,128]{2,1,0:T(8,128)(2,1)} %geo_ref.3) | copy-start | bytes 3145732
  20.3 30.8 %copy-start.5 = (bf16[256,2048]{1,0:T(8,128)(2,1)}, bf16[256,2048]{1,0:T(8,128)(2,1)S(1)}, u32[]{:S(2)}) copy-start(bf16[256,2048]{1,0:T(8,128)(2,1)S(1)} %get-tuple-element.217.signal_ref) | copy-start | bytes 3145732
  20.3 12.2 %all-to-all-start.1 = ((bf16[4,520,128]{2,1,0:T(8,128)(2,1)}), bf16[4,520,128]{2,1,0:T(8,128)(2,1)S(1)}, u32[]{:S(2)}, u32[]{:S(2)}) async-start(bf16[4,520,128]{2,1,0:T(8,128)(2,1)} %get-tuple-element.67), calls=%async_computation.1 | async-start | bytes 1064960 | tf_op jit(solution)/shard_map/all_to_all | solution.py:821
  33.2 36.8 %copy-start.9 = (s32[2]{0:T(128)S(1)}, s32[2]{0:T(128)}, u32[]{:S(2)}) copy-start(s32[2]{0:T(128)} %constant.114) | copy-start | bytes 28
  33.2 36.8 %copy-start.10 = (s32[2]{0:T(128)S(1)}, s32[2]{0:T(128)}, u32[]{:S(2)}) copy-start(s32[2]{0:T(128)} %constant.115) | copy-start | bytes 28
  33.2 11.5 %all-to-all-start.2 = ((bf16[4,136,128]{2,1,0:T(8,128)(2,1)}), bf16[4,136,128]{2,1,0:T(8,128)(2,1)S(1)}, u32[]{:S(2)}, u32[]{:S(2)}) async-start(bf16[4,136,128]{2,1,0:T(8,128)(2,1)} %fold.1), calls=%async_computation.2 | async-start | bytes 278528 | tf_op jit(solution)/shard_map/all_to_all | solution.py:821
  45.3 21.9 %all-to-all-start.3 = ((bf16[16,6,32,128]{3,2,1,0:T(8,128)(2,1)}), bf16[16,6,32,128]{3,2,1,0:T(8,128)(2,1)S(1)}, u32[]{:S(2)}, u32[]{:S(2)}) async-start(bf16[16,6,32,128]{3,2,1,0:T(8,128)(2,1)} %constant_dynamic-update-slice_fusion), calls=%async_computation.3 | async-start | bytes 1572864 | tf_op jit(solution)/shard_map/all_to_all | solution.py:821
  51.1 1.5 %collective-permute-start.3 = (s32[1,1]{1,0:T(1,128)}, s32[1,1]{1,0:T(1,128)}, u32[]{:S(2)}, u32[]{:S(2)}) collective-permute-start(s32[1,1]{1,0:T(1,128)} %slice.48), channel_id=1, source_target_pairs={{0,1},{1,0},{2,3},{3,2},{4,5},{5,4},{6,7},{7,6},{8,9},{9,8},{10,11... | collective-permute-start | bytes 20 | tf_op jit(solution)/shard_map/ppermute | solution.py:265
where the time goes:
time: 70.6 us; the launch traced here: 70 us
  waiting for transfers between devices  23.5 us (33%)
  Pallas kernels  22 us (31%)
  starting transfers between devices  16.9 us (24%)
  between operations  4.1 us (6%)
  local copies, waits for them, and re-layouts  3.48 us (5%)
    all_to_all x3, waiting for transfers between devices, exchange(): return lax.all_to_all(array, axes, split_axis=0, concat_axis=0, tiled=True)  23.5 us
    all_to_all x3, starting transfers between devices, exchange(): return lax.all_to_all(array, axes, split_axis=0, concat_axis=0, tiled=True)  13 us
    pallas_call x1, Pallas kernels, convolve_inner(): pl.pallas_call(functools.partial(inner_kernel, tuple(chunks)), out_shape=...  8.76 us
    pallas_call x1, Pallas kernels, convolve_edges(): pl.pallas_call(functools.partial(edge_kernel, planes), out_shape=(jax.Sha...  3.38 us
    ppermute x2, starting transfers between devices, wire_halo(): got.append(lax.ppermute(rows, 'wire', pairs + [(j, i) for i, j in pairs]))  3.32 us
    pallas_call x1, Pallas kernels, make_image(): pl.pallas_call(functools.partial(image_kernel, owner_total, share), out_s...  2.78 us
    pallas_call x1, Pallas kernels, prepare(): pl.pallas_call(functools.partial(prepare_kernel, planes, owner_total, sha...  1.94 us
    pallas_call x1, Pallas kernels, pack_tiles(): pl.pallas_call(functools.partial(pack_kernel, slots), out_shape=jax.Shape...  1.82 us
  transfers between devices with their start and end apart: 7, of which 3 were waited for; matrix products, arithmetic and copies ran while one was open for 3% of the time, Pallas kernels for 19%

commit v1 on v0

--- a/solution.py
+++ b/solution.py
@@ -168,10 +168,22 @@
     )(raw, chan_mask.reshape(wires // 128, 128), roi_owner[None], roi_block[None])
 
 
-def receive_kernel(owner_total, planes, share, wire_blocks, tick_blocks, rows_ref, own_ref, out_ref):
+def receive_kernel(owner_total, planes, share, wire_blocks, tick_blocks, own_ref, *refs):
+    pieces = refs[:-2]
+    out_ref, rows_ref = refs[-2:]
     lanes = lane_numbers()
     lane_f = lanes.astype(jnp.float32)
-    every = rows_ref[...]
+    place = lax.broadcasted_iota(jnp.int32, (owner_total, 128), 0)
+    shard = lax.axis_index("wire")
+    every = jnp.zeros((owner_total, 128), jnp.float32)
+    for step, ref in enumerate(pieces):
+        tags = ref[ref.shape[0] - TABLE :].astype(jnp.float32)
+        at = lax.bitwise_xor(shard, step) * planes
+        for plane in range(planes):
+            row = tags[2 * plane : 2 * plane + 1] * 128.0 + tags[2 * plane + 1 : 2 * plane + 2]
+            every = jnp.where(place == at + plane, row, every)
+    every = every.astype(jnp.int32)
+    rows_ref[...] = every
     owners = every >> 7
     own = own_ref[...]
     me = jnp.sum(jnp.where(lanes == 127, own & 127, 0).astype(jnp.float32), axis=1, keepdims=True)
@@ -246,15 +258,18 @@
     return (owner_total * share - tick_blocks) // GROUP + tick_blocks
 
 
-def make_receive_plan(rows, packed, owner_total, planes, share, wire_blocks, tick_blocks):
+def make_receive_plan(pieces, packed, owner_total, planes, share, wire_blocks, tick_blocks):
     return pl.pallas_call(
         functools.partial(receive_kernel, owner_total, planes, share, wire_blocks, tick_blocks),
-        out_shape=jax.ShapeDtypeStruct((8, 128), jnp.int32),
-        in_specs=[vmem(), vmem()],
-        out_specs=vmem(),
+        out_shape=(
+            jax.ShapeDtypeStruct((8, 128), jnp.int32),
+            jax.ShapeDtypeStruct((owner_total, 128), jnp.int32),
+        ),
+        in_specs=[vmem()] * (1 + len(pieces)),
+        out_specs=(vmem(), vmem()),
         compiler_params=pltpu.CompilerParams(vmem_limit_bytes=2 * MIB),
         name="receive_plan",
-    )(rows, packed)
+    )(packed, *pieces)
 
 
 def agree(rounds):
@@ -444,12 +459,10 @@
     band_ref,
     geo_ref,
     signal_ref,
-    partial_ref,
-    wide_ref,
-    lhs_ref,
-    out_ref,
-    turned_ref,
+    *refs,
 ):
+    part_refs = refs[:planes]
+    partial_ref, wide_ref, lhs_ref, out_ref, turned_ref = refs[planes:]
     wires, ticks = signal_ref.shape
     blocks = ticks // TB
     reach = band_ref.shape[0]
@@ -545,6 +558,9 @@
             partial_ref[plane, shard * cells : (shard + 1) * cells] = sums[
                 :, side * TB : (side + 1) * TB
             ]
+    mine = lax.axis_index("plane")
+    for step, ref in enumerate(part_refs):
+        ref[...] = partial_ref[lax.bitwise_xor(mine, step)]
 
 
 def convolve_edges(
@@ -555,16 +571,18 @@
     cells = geometry.shape[2]
     blocks = ticks // TB
     pitch = -(-(blocks + 2) // 8) * 8
+    height = blocks // planes * cells + TABLE
     flops = 2 * blocks * PAD * reach * 6 * TB * 2 * TB
     return pl.pallas_call(
         functools.partial(edge_kernel, planes),
         out_shape=(
             jax.ShapeDtypeStruct((wires, ticks), jnp.bfloat16),
-            jax.ShapeDtypeStruct((planes, blocks // planes * cells + TABLE, TB), jnp.bfloat16),
-        ),
+        )
+        + (jax.ShapeDtypeStruct((height, TB), jnp.bfloat16),) * planes,
         in_specs=[smem()] + [vmem()] * 10,
-        out_specs=(vmem(), vmem()),
+        out_specs=(vmem(),) * (1 + planes),
         scratch_shapes=[
+            pltpu.VMEM((planes, height, TB), jnp.bfloat16),
             pltpu.VMEM((2, 3 * PAD * pitch, TB), jnp.float32),
             pltpu.VMEM((2, PAD // 2 + reach - 1, blocks, 6 * TB), jnp.bfloat16),
             pltpu.VMEM((2, PAD * blocks, TB), jnp.float32),
@@ -576,36 +594,51 @@
     )(plan, own, inner, raw, mask, left, right, top, bottom, bands, geometry)
 
 
-def fold_kernel(pieces_ref, out_ref):
-    planes, height, _ = pieces_ref.shape
-    shards, lines, _ = out_ref.shape
+def fold_kernel(planes, *refs):
+    pieces = refs[:planes]
+    outs = refs[planes:-1]
+    sums_ref = refs[-1]
+    shards, lines, _ = sums_ref.shape
     cells = lines - TABLE
+    mine = lax.axis_index("plane")
     line = lax.broadcasted_iota(jnp.int32, (TABLE, 128), 0)
     table = jnp.zeros((TABLE, 128), jnp.float32)
-    for plane in range(planes):
-        tags = pieces_ref[plane, height - TABLE : height].astype(jnp.float32)
+    for step, ref in enumerate(pieces):
+        tags = ref[shards * cells :].astype(jnp.float32)
+        plane = lax.bitwise_xor(mine, step)
         table = jnp.where(line == 2 * plane, tags[0:1], table)
         table = jnp.where(line == 2 * plane + 1, tags[1:2], table)
     for shard in range(shards):
-        total = pieces_ref[0, shard * cells : (shard + 1) * cells].astype(jnp.float32)
-        for plane in range(1, planes):
-            total = total + pieces_ref[plane, shard * cells : (shard + 1) * cells].astype(
-                jnp.float32
-            )
-        out_ref[shard, 0:cells] = total.astype(jnp.bfloat16)
-        out_ref[shard, cells:lines] = table.astype(jnp.bfloat16)
+        total = jnp.zeros((cells, TB), jnp.float32)
+        for ref in pieces:
+            total = total + ref[shard * cells : (shard + 1) * cells].astype(jnp.float32)
+        sums_ref[shard, 0:cells] = total.astype(jnp.bfloat16)
+        sums_ref[shard, cells:lines] = table.astype(jnp.bfloat16)
+    mine = lax.axis_index("wire")
+    for step, ref in enumerate(outs):
+        ref[...] = sums_ref[lax.bitwise_xor(mine, step)]
 
 
 def fold(pieces, shards):
-    cells = (pieces.shape[1] - TABLE) // shards
+    cells = (pieces[0].shape[0] - TABLE) // shards
+    out = jax.ShapeDtypeStruct((cells + TABLE, TB), jnp.bfloat16)
     return pl.pallas_call(
-        fold_kernel,
-        out_shape=jax.ShapeDtypeStruct((shards, cells + TABLE, TB), jnp.bfloat16),
-        in_specs=[vmem()],
-        out_specs=vmem(),
+        functools.partial(fold_kernel, len(pieces)),
+        out_shape=(out,) * shards,
+        in_specs=[vmem()] * len(pieces),
+        out_specs=(vmem(),) * shards,
+        scratch_shapes=[pltpu.VMEM((shards, cells + TABLE, TB), jnp.bfloat16)],
         compiler_params=pltpu.CompilerParams(vmem_limit_bytes=4 * MIB),
         name="fold",
-    )(pieces)
+    )(*pieces)
+
+
+def swap_all(parts, axis):
+    got = [parts[0]]
+    for step in range(1, len(parts)):
+        pairs = [(i, i ^ step) for i in range(len(parts))]
+        got.append(lax.ppermute(parts[step], axis, pairs))
+    return got
 
 
 def pack_kernel(slots, plan_ref, signal_ref, payload_ref, tiles_ref):
@@ -839,26 +872,23 @@
     top, bottom = wire_halo(first, last, left, right)
     bands = make_bands(kernel[0])
     inner = convolve_inner(raw, mask, left, right, bands)
-    signal, partial = convolve_edges(
+    signal, *parts = convolve_edges(
         planes, send_plan, packed, inner, raw, mask, left, right, top, bottom, bands, geometry
     )
 
-    pieces = exchange(partial, "plane")
+    pieces = swap_all(parts, "plane")
     payload = pack_tiles(send_plan, signal, owner_total * share, block_wires)
     pieces, payload = lax.optimization_barrier((pieces, payload))
-    pieces = exchange(fold(pieces, wire_shards), "wire")
-
-    tables = pieces[:, cells : cells + 2 * planes].astype(jnp.int32)
-    tables = tables.reshape(owner_total, 2, 128)
-    rows = tables[:, 0] * 128 + tables[:, 1]
-    plan = make_receive_plan(
-        rows, packed, owner_total, planes, share, wires // block_wires, tick_blocks
+    pieces = swap_all(fold(pieces, wire_shards), "wire")
+
+    plan, rows = make_receive_plan(
+        pieces, packed, owner_total, planes, share, wires // block_wires, tick_blocks
     )
     staged = stage_geometry(
         plan, geometry, group_total(owner_total, share, tick_blocks), owner_total * share
     )
 
-    sums = jnp.sum(pieces[:, :cells].astype(jnp.float32), axis=0).astype(jnp.bfloat16)
+    sums = sum(piece[:cells].astype(jnp.float32) for piece in pieces).astype(jnp.bfloat16)
     payload = lax.dynamic_update_slice(
         payload.reshape(owner_total, share, block_wires, TB),
         sums.reshape(1, cells // block_wires, block_wires, TB),

time: 70.6 us -> 66.1 us (0.936)
  waiting for transfers between devices: 23.5 us -> 18.9 us
  starting transfers between devices: 16.9 us -> 18.8 us
  Pallas kernels: 22 us -> 20.5 us
    ppermute x0 -> x6, starting transfers between devices: none -> 10.2 us  [swap_all(): got.append(lax.ppermute(parts[step], axis, pairs))]
    all_to_all x3 -> x1, waiting for transfers between devices: 23.5 us -> 13.6 us  [exchange(): return lax.all_to_all(array, axes, split_axis=0, concat_axis=0, tiled=True)]
    all_to_all x3 -> x1, starting transfers between devices: 13 us -> 4.81 us  [exchange(): return lax.all_to_all(array, axes, split_axis=0, concat_axis=0, tiled=True)]
    ppermute x0 -> x6, waiting for transfers between devices: none -> 5.25 us  [swap_all(): got.append(lax.ppermute(parts[step], axis, pairs))]
    pallas_call x1, Pallas kernels: 3.38 us -> 2.62 us  [convolve_edges(): pl.pallas_call(functools.partial(edge_kernel, planes), out_shape=(jax.Sha...]
  transfers between devices with their start and end apart: 7 -> 11, of which waited for: 3 -> 4; matrix products, arithmetic and copies ran while one was open for 3% -> 3% of each run, Pallas kernels for 19% -> 20%
where the time goes in v1:
time: 66.1 us; the launch traced here: 65.7 us
  Pallas kernels  20.5 us (31%)
  waiting for transfers between devices  18.9 us (29%)
  starting transfers between devices  18.8 us (28%)
  between operations  3.98 us (6%)
  local copies, waits for them, and re-layouts  3.45 us (5%)
    all_to_all x1, waiting for transfers between devices, exchange(): return lax.all_to_all(array, axes, split_axis=0, concat_axis=0, tiled=True)  13.6 us
    ppermute x6, starting transfers between devices, swap_all(): got.append(lax.ppermute(parts[step], axis, pairs))  10.2 us
    pallas_call x1, Pallas kernels, convolve_inner(): pl.pallas_call(functools.partial(inner_kernel, tuple(chunks)), out_shape=...  8.77 us
    ppermute x6, waiting for transfers between devices, swap_all(): got.append(lax.ppermute(parts[step], axis, pairs))  5.25 us
    all_to_all x1, starting transfers between devices, exchange(): return lax.all_to_all(array, axes, split_axis=0, concat_axis=0, tiled=True)  4.81 us
    ppermute x2, starting transfers between devices, wire_halo(): got.append(lax.ppermute(rows, 'wire', pairs + [(j, i) for i, j in pairs]))  3.32 us
    pallas_call x1, Pallas kernels, convolve_edges(): pl.pallas_call(functools.partial(edge_kernel, planes), out_shape=(jax.Sha...  2.62 us
    pallas_call x1, Pallas kernels, make_image(): pl.pallas_call(functools.partial(image_kernel, owner_total, share), out_s...  2.6 us
  transfers between devices with their start and end apart: 11, of which 4 were waited for; matrix products, arithmetic and copies ran while one was open for 3% of the time, Pallas kernels for 20%

profile of v1, /device:TPU:0, one launch (start us, length us, event | category | flops | bytes accessed | tf_op | source)
XLA Modules:
  0.0 65.7 jit_solution(8921011528207949875)
XLA Ops:
  0.6 1.9 %prepare.1 = (bf16[256,128]{1,0:T(8,128)(2,1)}, bf16[16,2048]{1,0:T(8,128)(2,1)}, bf16[16,2048]{1,0:T(8,128)(2,1)}, s32[1,128]{1,0:T(1,128)S(1)}, s32[8,128]{1,0:T(8,128)}, /*index=5*/bf16[256,128]{1,0:T(8,128)(2,1)}) custom-call(bf16[256,2048]{1,0:T(8,128)(2,1)} %raw_ref.3, s32[2,128]{1,0:T(2,128)} %bitcast.97, s32[1,102]{1,0:T(1,128)} %bitcast.98, ...), custom_call_target="tpu_custom_call" | custom-call | tf_op jit(solution)/shard_map/prepare/pallas_call | solution.py:156
  3.1 0.7 %copy-done.3 = bf16[1,21,256]{2,1,0:T(8,128)(2,1)S(1)} copy-done((bf16[1,21,256]{2,1,0:T(8,128)(2,1)S(1)}, bf16[1,21,256]{2,1,0:T(8,128)(2,1)}, u32[]{:S(2)}) %copy-start.3) | copy-done | bytes 10776
  3.8 0.6 bands.1.band_ref
  4.7 2.7 %collective-permute-start.1 = (bf16[16,2304]{1,0:T(8,128)(2,1)S(1)}, bf16[16,2304]{1,0:T(8,128)(2,1)S(1)}, u32[]{:S(2)}, u32[]{:S(2)}) collective-permute-start(bf16[16,2304]{1,0:T(8,128)(2,1)S(1)} %get-tuple-element.153), channel_id=1, source_target_pairs={{0,2},{4,6},{2,0},{6,4},{1,3},{5,7},{3,1},{7,5},{8,10},{12,14},{10... | collective-permute-start | bytes 221192 | tf_op jit(solution)/shard_map/ppermute | solution.py:849
  7.4 0.7 collective-permute-start.2
  8.1 8.8 %inner.1.inner_ref = bf16[224,2048]{1,0:T(8,128)(2,1)S(1)} custom-call(bf16[256,2048]{1,0:T(8,128)(2,1)S(1)} %copy-done, bf16[256,128]{1,0:T(8,128)(2,1)S(1)} %copy-done.1, bf16[256,128]{1,0:T(8,128)(2,1)S(1)} %get-tuple-element.159.left_ref, bf16[256,128]{1,0:T(8,128)(2,1)S(1)} %get-tuple-element.158.right_ref, bf16[11,768,256]{2,1,0:T(8,128)(2,1)S(1)} %bands.1.band_ref), custom_call_target="tpu_custom_call" | custom-call | flops 7751073792 | bytes 6291456 | tf_op jit(solution)/shard_map/inner/pallas_call | solution.py:432
  16.9 2.6 %edges.1 = (bf16[256,2048]{1,0:T(8,128)(2,1)S(1)}, bf16[520,128]{1,0:T(8,128)(2,1)S(1)}, bf16[520,128]{1,0:T(8,128)(2,1)S(1)}, bf16[520,128]{1,0:T(8,128)(2,1)S(1)}, bf16[520,128]{1,0:T(8,128)(2,1)S(1)}) custom-call(s32[8,128]{1,0:T(8,128)S(1)} %copy-done.2, s32[1,128]{1,0:T(1,128)S(1)} %get-tuple-element.241.own_ref, bf16[224,2048]{1,0:T(8,128)(2,1)S(1)} %inner.1.inner_ref, ...), custom_call_target="tpu_custom_call" | custom-call | flops 1107296256 | bytes 6291456 | tf_op jit(solution)/shard_map/edges/pallas_call | solution.py:576
  19.6 1.6 %collective-permute-start.3 = (bf16[520,128]{1,0:T(8,128)(2,1)S(1)}, bf16[520,128]{1,0:T(8,128)(2,1)S(1)}, u32[]{:S(2)}, u32[]{:S(2)}) collective-permute-start(bf16[520,128]{1,0:T(8,128)(2,1)S(1)} %get-tuple-element.80), channel_id=1, source_target_pairs={{0,8},{8,0},{16,24},{24,16},{1,9},{9,1},{17,25},{25,17},{2,10},{10... | collective-permute-start | bytes 399368 | tf_op jit(solution)/shard_map/ppermute | solution.py:640
  21.1 1.5 %collective-permute-start.4 = (bf16[520,128]{1,0:T(8,128)(2,1)S(1)}, bf16[520,128]{1,0:T(8,128)(2,1)S(1)}, u32[]{:S(2)}, u32[]{:S(2)}) collective-permute-start(bf16[520,128]{1,0:T(8,128)(2,1)S(1)} %get-tuple-element.81), channel_id=1, source_target_pairs={{0,16},{8,24},{16,0},{24,8},{1,17},{9,25},{17,1},{25,9},{2,18},{10... | collective-permute-start | bytes 399368 | tf_op jit(solution)/shard_map/ppermute | solution.py:640
  23.1 1.8 %pack.1 = bf16[96,32,128]{2,1,0:T(8,128)(2,1)} custom-call(s32[8,128]{1,0:T(8,128)S(1)} %copy-done.2, bf16[256,2048]{1,0:T(8,128)(2,1)S(1)} %get-tuple-element.239.signal_ref), custom_call_target="tpu_custom_call" | custom-call | flops 100000000 | bytes 3145728 | tf_op jit(solution)/shard_map/pack/pallas_call | solution.py:659
  24.9 0.7 %collective-permute-done.3.refs_1_ = bf16[520,128]{1,0:T(8,128)(2,1)S(1)} collective-permute-done((bf16[520,128]{1,0:T(8,128)(2,1)S(1)}, bf16[520,128]{1,0:T(8,128)(2,1)S(1)}, u32[]{:S(2)}, u32[]{:S(2)}) %collective-permute-start.3) | collective-permute-done | bytes 133152 | tf_op jit(solution)/shard_map/ppermute | solution.py:640
  25.7 3.7 %collective-permute-done.4.refs_2_ = bf16[520,128]{1,0:T(8,128)(2,1)S(1)} collective-permute-done((bf16[520,128]{1,0:T(8,128)(2,1)S(1)}, bf16[520,128]{1,0:T(8,128)(2,1)S(1)}, u32[]{:S(2)}, u32[]{:S(2)}) %collective-permute-start.4) | collective-permute-done | bytes 133152 | tf_op jit(solution)/shard_map/ppermute | solution.py:640
  29.5 4.2 %collective-permute-start.6 = (bf16[136,128]{1,0:T(8,128)(2,1)S(1)}, bf16[136,128]{1,0:T(8,128)(2,1)S(1)}, u32[]{:S(2)}, u32[]{:S(2)}) collective-permute-start(bf16[136,128]{1,0:T(8,128)(2,1)S(1)} %get-tuple-element.88), channel_id=1, source_target_pairs={{0,2},{2,0},{4,6},{6,4},{1,3},{3,1},{5,7},{7,5},{8,10},{10,8},{12,... | collective-permute-start | bytes 104456 | tf_op jit(solution)/shard_map/ppermute | solution.py:640
  33.6 2.4 %collective-permute-start.8 = (bf16[136,128]{1,0:T(8,128)(2,1)S(1)}, bf16[136,128]{1,0:T(8,128)(2,1)S(1)}, u32[]{:S(2)}, u32[]{:S(2)}) collective-permute-start(bf16[136,128]{1,0:T(8,128)(2,1)S(1)} %get-tuple-element.90), channel_id=1, source_target_pairs={{0,6},{2,4},{4,2},{6,0},{1,7},{3,5},{5,3},{7,1},{8,14},{10,12},{12... | collective-permute-start | bytes 104456 | tf_op jit(solution)/shard_map/ppermute | solution.py:640
  36.1 0.6 slice.47
  38.5 0.8 %collective-permute-done.8.refs_3_ = bf16[136,128]{1,0:T(8,128)(2,1)S(1)} collective-permute-done((bf16[136,128]{1,0:T(8,128)(2,1)S(1)}, bf16[136,128]{1,0:T(8,128)(2,1)S(1)}, u32[]{:S(2)}, u32[]{:S(2)}) %collective-permute-start.8) | collective-permute-done | bytes 34848 | tf_op jit(solution)/shard_map/ppermute | solution.py:640
  39.4 0.6 constant_dynamic-update-slice_fusion
  40.0 4.8 %all-to-all-start.1 = ((bf16[16,6,32,128]{3,2,1,0:T(8,128)(2,1)}), bf16[16,6,32,128]{3,2,1,0:T(8,128)(2,1)S(1)}, u32[]{:S(2)}, u32[]{:S(2)}) async-start(bf16[16,6,32,128]{3,2,1,0:T(8,128)(2,1)} %constant_dynamic-update-slice_fusion), calls=%async_computation.1 | async-start | bytes 1572864 | tf_op jit(solution)/shard_map/all_to_all | solution.py:854
  44.8 0.6 receive_plan.1
  45.4 0.6 slice.48
  46.0 0.7 %copy.29 = s32[16,128]{0,1:T(8,128)} copy(s32[16,128]{1,0:T(8,128)S(1)} %get-tuple-element.123) | data formatting | bytes 16384 | tf_op jit(solution)/shard_map/while | solution.py:901
  46.7 1.4 %stage.1.staged_ref = bf16[26,128,256]{2,1,0:T(8,128)(2,1)S(1)} custom-call(s32[8,128]{1,0:T(8,128)S(1)} %get-tuple-element.242.plan_ref, bf16[128,32,128]{2,1,0:T(8,128)(2,1)S(1)} %copy-done.4), custom_call_target="tpu_custom_call" | custom-call | flops 100000000 | bytes 3145728 | tf_op jit(solution)/shard_map/stage/pallas_call | solution.py:683
  49.5 13.6 %all-to-all-done.1 = bf16[16,6,32,128]{3,2,1,0:T(8,128)(2,1)S(1)} async-done(((bf16[16,6,32,128]{3,2,1,0:T(8,128)(2,1)}), bf16[16,6,32,128]{3,2,1,0:T(8,128)(2,1)S(1)}, u32[]{:S(2)}, u32[]{:S(2)}) %all-to-all-start.1) | async-done | bytes 786464 | tf_op jit(solution)/shard_map/all_to_all | solution.py:854
  63.1 2.6 %image.1 = f32[128,2048]{1,0:T(8,128)} custom-call(s32[8,128]{1,0:T(8,128)S(1)} %get-tuple-element.242.plan_ref, bf16[96,32,128]{2,1,0:T(8,128)(2,1)S(1)} %bitcast.89, bf16[26,128,256]{2,1,0:T(8,128)(2,1)S(1)} %stage.1.staged_ref), custom_call_target="tpu_custom_call" | custom-call | flops 100000000 | bytes 3145728 | tf_op jit(solution)/shard_map/image/pallas_call | solution.py:732
  (37 shorter events, 1.4 us)
Async XLA Ops:
  0.6 7.4 %copy-start = (bf16[256,2048]{1,0:T(8,128)(2,1)S(1)}, bf16[256,2048]{1,0:T(8,128)(2,1)}, u32[]{:S(2)}) copy-start(bf16[256,2048]{1,0:T(8,128)(2,1)} %raw_ref.3) | copy-start | bytes 3145732
  2.6 5.5 %copy-start.1 = (bf16[256,128]{1,0:T(8,128)(2,1)S(1)}, bf16[256,128]{1,0:T(8,128)(2,1)}, u32[]{:S(2)}) copy-start(bf16[256,128]{1,0:T(8,128)(2,1)} %get-tuple-element.74.mask_ref) | copy-start | bytes 196612
  2.6 1.9 %collective-permute-start = (bf16[256,128]{1,0:T(8,128)(2,1)}, bf16[256,128]{1,0:T(8,128)(2,1)S(1)}, u32[]{:S(2)}, u32[]{:S(2)}) collective-permute-start(bf16[256,128]{1,0:T(8,128)(2,1)} %get-tuple-element.75), channel_id=1, source_target_pairs={{0,1},{1,0},{2,3},{3,2},{4,5},{5,4},{6,7},{7,6},{8,9},{9,8},{10,11... | collective-permute-start | bytes 196616 | tf_op jit(solution)/shard_map/ppermute | solution.py:833
  3.1 0.7 %copy-start.3 = (bf16[1,21,256]{2,1,0:T(8,128)(2,1)S(1)}, bf16[1,21,256]{2,1,0:T(8,128)(2,1)}, u32[]{:S(2)}) copy-start(bf16[1,21,256]{2,1,0:T(8,128)(2,1)} %param.10) | copy-start | bytes 32260
  3.8 0.8 %copy-start.7 = (bf16[16,2048]{1,0:T(8,128)(2,1)S(1)}, bf16[16,2048]{1,0:T(8,128)(2,1)}, u32[]{:S(2)}) copy-start(bf16[16,2048]{1,0:T(8,128)(2,1)} %get-tuple-element.76) | copy-start | bytes 196612
  3.8 0.9 %copy-start.8 = (bf16[16,2048]{1,0:T(8,128)(2,1)S(1)}, bf16[16,2048]{1,0:T(8,128)(2,1)}, u32[]{:S(2)}) copy-start(bf16[16,2048]{1,0:T(8,128)(2,1)} %get-tuple-element.77) | copy-start | bytes 196612
  4.7 12.2 %collective-permute-start.1 = (bf16[16,2304]{1,0:T(8,128)(2,1)S(1)}, bf16[16,2304]{1,0:T(8,128)(2,1)S(1)}, u32[]{:S(2)}, u32[]{:S(2)}) collective-permute-start(bf16[16,2304]{1,0:T(8,128)(2,1)S(1)} %get-tuple-element.153), channel_id=1, source_target_pairs={{0,2},{4,6},{2,0},{6,4},{1,3},{5,7},{3,1},{7,5},{8,10},{12,14},{10... | collective-permute-start | bytes 221192 | tf_op jit(solution)/shard_map/ppermute | solution.py:849
  7.4 9.5 %collective-permute-start.2 = (bf16[16,2304]{1,0:T(8,128)(2,1)S(1)}, bf16[16,2304]{1,0:T(8,128)(2,1)S(1)}, u32[]{:S(2)}, u32[]{:S(2)}) collective-permute-start(bf16[16,2304]{1,0:T(8,128)(2,1)S(1)} %get-tuple-element.152), channel_id=1, source_target_pairs={{2,4},{4,2},{3,5},{5,3},{10,12},{12,10},{11,13},{13,11},{18,20},{2... | collective-permute-start | bytes 221192 | tf_op jit(solution)/shard_map/ppermute | solution.py:849
  8.1 8.8 %copy-start.2 = (s32[8,128]{1,0:T(8,128)S(1)}, s32[8,128]{1,0:T(8,128)}, u32[]{:S(2)}) copy-start(s32[8,128]{1,0:T(8,128)} %get-tuple-element.72.plan_ref) | copy-start | bytes 12292
  8.1 8.8 %copy-start.4 = (bf16[128,32,128]{2,1,0:T(8,128)(2,1)S(1)}, bf16[128,32,128]{2,1,0:T(8,128)(2,1)}, u32[]{:S(2)}) copy-start(bf16[128,32,128]{2,1,0:T(8,128)(2,1)} %geo_ref.3) | copy-start | bytes 3145732
  19.6 20.5 %copy-start.5 = (bf16[256,2048]{1,0:T(8,128)(2,1)}, bf16[256,2048]{1,0:T(8,128)(2,1)S(1)}, u32[]{:S(2)}) copy-start(bf16[256,2048]{1,0:T(8,128)(2,1)S(1)} %get-tuple-element.239.signal_ref) | copy-start | bytes 3145732
  19.6 6.1 %collective-permute-start.3 = (bf16[520,128]{1,0:T(8,128)(2,1)S(1)}, bf16[520,128]{1,0:T(8,128)(2,1)S(1)}, u32[]{:S(2)}, u32[]{:S(2)}) collective-permute-start(bf16[520,128]{1,0:T(8,128)(2,1)S(1)} %get-tuple-element.80), channel_id=1, source_target_pairs={{0,8},{8,0},{16,24},{24,16},{1,9},{9,1},{17,25},{25,17},{2,10},{10... | collective-permute-start | bytes 399368 | tf_op jit(solution)/shard_map/ppermute | solution.py:640
  21.1 8.2 %collective-permute-start.4 = (bf16[520,128]{1,0:T(8,128)(2,1)S(1)}, bf16[520,128]{1,0:T(8,128)(2,1)S(1)}, u32[]{:S(2)}, u32[]{:S(2)}) collective-permute-start(bf16[520,128]{1,0:T(8,128)(2,1)S(1)} %get-tuple-element.81), channel_id=1, source_target_pairs={{0,16},{8,24},{16,0},{24,8},{1,17},{9,25},{17,1},{25,9},{2,18},{10... | collective-permute-start | bytes 399368 | tf_op jit(solution)/shard_map/ppermute | solution.py:640
  22.7 6.7 %collective-permute-start.5 = (bf16[520,128]{1,0:T(8,128)(2,1)S(1)}, bf16[520,128]{1,0:T(8,128)(2,1)S(1)}, u32[]{:S(2)}, u32[]{:S(2)}) collective-permute-start(bf16[520,128]{1,0:T(8,128)(2,1)S(1)} %get-tuple-element.82), channel_id=1, source_target_pairs={{0,24},{8,16},{16,8},{24,0},{1,25},{9,17},{17,9},{25,1},{2,26},{10... | collective-permute-start | bytes 399368 | tf_op jit(solution)/shard_map/ppermute | solution.py:640
  29.4 36.3 %copy-start.9 = (s32[2]{0:T(128)S(1)}, s32[2]{0:T(128)}, u32[]{:S(2)}) copy-start(s32[2]{0:T(128)} %constant.110) | copy-start | bytes 28
  29.4 36.3 %copy-start.10 = (s32[2]{0:T(128)S(1)}, s32[2]{0:T(128)}, u32[]{:S(2)}) copy-start(s32[2]{0:T(128)} %constant.111) | copy-start | bytes 28
  29.5 9.1 %collective-permute-start.6 = (bf16[136,128]{1,0:T(8,128)(2,1)S(1)}, bf16[136,128]{1,0:T(8,128)(2,1)S(1)}, u32[]{:S(2)}, u32[]{:S(2)}) collective-permute-start(bf16[136,128]{1,0:T(8,128)(2,1)S(1)} %get-tuple-element.88), channel_id=1, source_target_pairs={{0,2},{2,0},{4,6},{6,4},{1,3},{3,1},{5,7},{7,5},{8,10},{10,8},{12,... | collective-permute-start | bytes 104456 | tf_op jit(solution)/shard_map/ppermute | solution.py:640
  33.6 4.9 %collective-permute-start.7 = (bf16[136,128]{1,0:T(8,128)(2,1)S(1)}, bf16[136,128]{1,0:T(8,128)(2,1)S(1)}, u32[]{:S(2)}, u32[]{:S(2)}) collective-permute-start(bf16[136,128]{1,0:T(8,128)(2,1)S(1)} %get-tuple-element.89), channel_id=1, source_target_pairs={{0,4},{2,6},{4,0},{6,2},{1,5},{3,7},{5,1},{7,3},{8,12},{10,14},{12... | collective-permute-start | bytes 104456 | tf_op jit(solution)/shard_map/ppermute | solution.py:640
  33.6 5.7 %collective-permute-start.8 = (bf16[136,128]{1,0:T(8,128)(2,1)S(1)}, bf16[136,128]{1,0:T(8,128)(2,1)S(1)}, u32[]{:S(2)}, u32[]{:S(2)}) collective-permute-start(bf16[136,128]{1,0:T(8,128)(2,1)S(1)} %get-tuple-element.90), channel_id=1, source_target_pairs={{0,6},{2,4},{4,2},{6,0},{1,7},{3,5},{5,3},{7,1},{8,14},{10,12},{12... | collective-permute-start | bytes 104456 | tf_op jit(solution)/shard_map/ppermute | solution.py:640
  40.0 23.1 %all-to-all-start.1 = ((bf16[16,6,32,128]{3,2,1,0:T(8,128)(2,1)}), bf16[16,6,32,128]{3,2,1,0:T(8,128)(2,1)S(1)}, u32[]{:S(2)}, u32[]{:S(2)}) async-start(bf16[16,6,32,128]{3,2,1,0:T(8,128)(2,1)} %constant_dynamic-update-slice_fusion), calls=%async_computation.1 | async-start | bytes 1572864 | tf_op jit(solution)/shard_map/all_to_all | solution.py:854
  46.0 2.2 %collective-permute-start.9 = (s32[1,1]{1,0:T(1,128)}, s32[1,1]{1,0:T(1,128)}, u32[]{:S(2)}, u32[]{:S(2)}) collective-permute-start(s32[1,1]{1,0:T(1,128)} %slice.48), channel_id=1, source_target_pairs={{0,1},{1,0},{2,3},{3,2},{4,5},{5,4},{6,7},{7,6},{8,9},{9,8},{10,11... | collective-permute-start | bytes 20 | tf_op jit(solution)/shard_map/ppermute | solution.py:280

commit v2 on v1

--- a/solution.py
+++ b/solution.py
@@ -118,7 +118,8 @@
     rows = lax.broadcasted_iota(jnp.int32, (owner_total, 128), 0)
     member = (own >> 7) == rows
     rank = count_before(member, earlier_lanes())
-    place = jnp.where(rank < share, rows.astype(jnp.float32) * share + rank, -1.0)
+    step = lax.bitwise_xor(rows, jnp.full_like(rows, me)).astype(jnp.float32)
+    place = jnp.where(rank < share, step * share + rank, -1.0)
     place = jnp.where(rows.astype(jnp.float32) == hot, -2.0, place)
     place = jnp.sum(jnp.where(member, place + 3.0, 0.0), axis=0, keepdims=True)
 
@@ -634,10 +635,14 @@
 
 
 def swap_all(parts, axis):
-    got = [parts[0]]
-    for step in range(1, len(parts)):
-        pairs = [(i, i ^ step) for i in range(len(parts))]
-        got.append(lax.ppermute(parts[step], axis, pairs))
+    got = [parts[0]] * len(parts)
+    for step in reversed(range(1, len(parts))):
+        other = step
+        if axis == ("plane", "wire"):
+            planes = lax.axis_size("plane")
+            other = step % planes * lax.axis_size("wire") + step // planes
+        pairs = [(i, i ^ other) for i in range(len(parts))]
+        got[step] = lax.ppermute(parts[step], axis, pairs)
     return got
 
 
@@ -668,6 +673,36 @@
     )(plan, signal)
 
 
+def place_kernel(shards, share, plan_ref, tiles_ref, *refs):
+    pieces = refs[:shards]
+    outs = refs[shards:]
+    block_wires = tiles_ref.shape[1]
+    cells = pieces[0].shape[0] - TABLE
+    total = jnp.zeros((cells, TB), jnp.float32)
+    for ref in pieces:
+        total = total + ref[0:cells].astype(jnp.float32)
+    sums = total.astype(jnp.bfloat16).reshape(cells // block_wires, block_wires, TB)
+    hot = lax.bitwise_xor(plan_ref[1, 0], plan_ref[1, 2])
+    for step, ref in enumerate(outs):
+        ref[...] = tiles_ref[step * share : (step + 1) * share]
+
+        @pl.when(hot == step)
+        def _(ref=ref):
+            ref[0 : cells // block_wires] = sums
+
+
+def place_sums(plan, tiles, pieces, owner_total, share):
+    out = jax.ShapeDtypeStruct((share,) + tiles.shape[1:], tiles.dtype)
+    return pl.pallas_call(
+        functools.partial(place_kernel, len(pieces), share),
+        out_shape=(out,) * owner_total,
+        in_specs=[smem()] + [vmem()] * (1 + len(pieces)),
+        out_specs=(vmem(),) * owner_total,
+        compiler_params=pltpu.CompilerParams(vmem_limit_bytes=6 * MIB),
+        name="place",
+    )(plan, tiles, *pieces)
+
+
 def stage_kernel(slots, plan_ref, geo_ref, out_ref, rows_ref):
     groups = out_ref.shape[0]
     rows_ref[...] = jnp.zeros_like(rows_ref)
@@ -692,20 +727,22 @@
     )(plan, geometry)
 
 
-def image_kernel(owner_total, share, plan_ref, arrived_ref, staged_ref, image_ref, tiles_ref):
+def image_kernel(owner_total, share, plan_ref, staged_ref, *refs):
+    arrived = refs[:owner_total]
+    image_ref, tiles_ref = refs[owner_total:]
     cells, ticks = image_ref.shape
-    block_wires = arrived_ref.shape[1]
+    block_wires = arrived[0].shape[1]
     groups = staged_ref.shape[0]
-    is_hot = plan_ref[1, 0] == plan_ref[1, 2]
+    me = plan_ref[1, 2]
+    is_hot = plan_ref[1, 0] == me
     counts = plan_ref[1, 3] == 1
 
     @pl.when(is_hot)
     def _():
-        for source in range(owner_total):
-            sums = arrived_ref[source * share : source * share + cells // block_wires]
-            image_ref[:, source * TB : (source + 1) * TB] = sums.reshape(cells, TB).astype(
-                jnp.float32
-            )
+        for step, ref in enumerate(arrived):
+            at = pl.multiple_of(lax.bitwise_xor(me, step) * TB, TB)
+            sums = ref[0 : cells // block_wires]
+            image_ref[:, pl.ds(at, TB)] = sums.reshape(cells, TB).astype(jnp.float32)
 
     @pl.when(jnp.logical_not(is_hot))
     def _():
@@ -714,8 +751,10 @@
 
         @pl.when(counts)
         def _():
-            for slot in range(owner_total * share):
-                tiles_ref[plan_ref[0, slot]] = arrived_ref[slot]
+            for step, ref in enumerate(arrived):
+                source = lax.bitwise_xor(me, step)
+                for slot in range(share):
+                    tiles_ref[plan_ref[0, source * share + slot]] = ref[slot]
             for group in range(groups):
                 tiles = tiles_ref[group * GROUP : (group + 1) * GROUP]
                 at = pl.ds(pl.multiple_of(plan_ref[3, group] * TB, TB), TB)
@@ -726,13 +765,13 @@
                 )
 
 
-def make_image(plan, arrived, staged, owner_total, share, ticks):
+def make_image(plan, arrived, staged, share, ticks):
     groups, cells, _ = staged.shape
-    block_wires = arrived.shape[1]
-    return pl.pallas_call(
-        functools.partial(image_kernel, owner_total, share),
+    block_wires = arrived[0].shape[1]
+    return pl.pallas_call(
+        functools.partial(image_kernel, len(arrived), share),
         out_shape=jax.ShapeDtypeStruct((cells, ticks), jnp.float32),
-        in_specs=[smem(), vmem(), vmem()],
+        in_specs=[smem()] + [vmem()] * (1 + len(arrived)),
         out_specs=vmem(),
         scratch_shapes=[
             pltpu.VMEM((groups * GROUP + 1, block_wires, TB), jnp.bfloat16),
@@ -740,7 +779,7 @@
         cost_estimate=pl.CostEstimate(flops=10**8, bytes_accessed=3 * MIB, transcendentals=0),
         compiler_params=pltpu.CompilerParams(vmem_limit_bytes=16 * MIB),
         name="image",
-    )(plan, arrived, staged)
+    )(plan, staged, *arrived)
 
 
 def more_kernel(owner_total, planes, share, plan_ref, table_ref, arrived_ref, geo_ref, before_ref, image_ref):
@@ -888,14 +927,9 @@
         plan, geometry, group_total(owner_total, share, tick_blocks), owner_total * share
     )
 
-    sums = sum(piece[:cells].astype(jnp.float32) for piece in pieces).astype(jnp.bfloat16)
-    payload = lax.dynamic_update_slice(
-        payload.reshape(owner_total, share, block_wires, TB),
-        sums.reshape(1, cells // block_wires, block_wires, TB),
-        (send_plan[1, 0], 0, 0, 0),
-    )
-    arrived = exchange(payload).reshape(owner_total * share, block_wires, TB)
-    image = make_image(plan, arrived, staged, owner_total, share, ticks)
+    payload = place_sums(send_plan, payload, pieces, owner_total, share)
+    arrived = swap_all(payload, ("plane", "wire"))
+    image = make_image(plan, arrived, staged, share, ticks)
 
     trips = agree(plan[1:2, 1:2])[0, 0]
     image = lax.fori_loop(

time: 66.1 us -> 76.6 us (1.16)
  starting transfers between devices: 18.8 us -> 40.5 us
  waiting for transfers between devices: 18.9 us -> 9.93 us
  local copies, waits for them, and re-layouts: 3.45 us -> 1.62 us
  between operations: 3.98 us -> 2.21 us
  Pallas kernels: 20.5 us -> 22.1 us
    ppermute x6 -> x21, starting transfers between devices: 10.2 us -> 36.6 us  [swap_all(): got[step] = lax.ppermute(parts[step], axis, pairs)]
    all_to_all x1 -> x0, waiting for transfers between devices: 13.6 us -> none  [exchange(): return lax.all_to_all(array, axes, split_axis=0, concat_axis=0, tiled=True)]
    all_to_all x1 -> x0, starting transfers between devices: 4.81 us -> none  [exchange(): return lax.all_to_all(array, axes, split_axis=0, concat_axis=0, tiled=True)]
    ppermute x6 -> x21, waiting for transfers between devices: 5.25 us -> 9.92 us  [swap_all(): got[step] = lax.ppermute(parts[step], axis, pairs)]
    pallas_call x1 -> x2, Pallas kernels: 2.6 us -> 3.51 us  [the longest x1 2.64 us: make_image(): pl.pallas_call(functools.partial(image_kernel, len(arrived), share), out_...]
    pallas_call x1, Pallas kernels: 2.62 us -> 3.48 us  [convolve_edges(): pl.pallas_call(functools.partial(edge_kernel, planes), out_shape=(jax.Sha...]
  transfers between devices with their start and end apart: 11 -> 25, of which waited for: 4 -> 5; matrix products, arithmetic and copies ran while one was open for 3% -> 1% of each run, Pallas kernels for 20% -> 17%
where the time goes in v2:
time: 76.6 us; the launch traced here: 76.3 us
  starting transfers between devices  40.5 us (53%)
  Pallas kernels  22.1 us (29%)
  waiting for transfers between devices  9.93 us (13%)
  between operations  2.21 us (3%)
  local copies, waits for them, and re-layouts  1.62 us (2%)
    ppermute x21, starting transfers between devices, swap_all(): got[step] = lax.ppermute(parts[step], axis, pairs)  36.6 us
    ppermute x21, waiting for transfers between devices, swap_all(): got[step] = lax.ppermute(parts[step], axis, pairs)  9.92 us
    pallas_call x1, Pallas kernels, convolve_inner(): pl.pallas_call(functools.partial(inner_kernel, tuple(chunks)), out_shape=...  8.84 us
    pallas_call x1, Pallas kernels, convolve_edges(): pl.pallas_call(functools.partial(edge_kernel, planes), out_shape=(jax.Sha...  3.48 us
    ppermute x2, starting transfers between devices, wire_halo(): got.append(lax.ppermute(rows, 'wire', pairs + [(j, i) for i, j in pairs]))  3.32 us
    pallas_call x1, Pallas kernels, make_image(): pl.pallas_call(functools.partial(image_kernel, len(arrived), share), out_...  2.64 us
    pallas_call x1, Pallas kernels, prepare(): pl.pallas_call(functools.partial(prepare_kernel, planes, owner_total, sha...  1.93 us
    pallas_call x1, Pallas kernels, pack_tiles(): pl.pallas_call(functools.partial(pack_kernel, slots), out_shape=jax.Shape...  1.57 us
  transfers between devices with their start and end apart: 25, of which 5 were waited for; matrix products, arithmetic and copies ran while one was open for 1% of the time, Pallas kernels for 17%

profile of v2, /device:TPU:0, one launch (start us, length us, event | category | flops | bytes accessed | tf_op | source)
XLA Modules:
  0.0 76.3 jit_solution(10627094634175068053)
XLA Ops:
  0.6 1.9 %prepare.1 = (bf16[256,128]{1,0:T(8,128)(2,1)}, bf16[16,2048]{1,0:T(8,128)(2,1)}, bf16[16,2048]{1,0:T(8,128)(2,1)}, s32[1,128]{1,0:T(1,128)S(1)}, s32[8,128]{1,0:T(8,128)}, /*index=5*/bf16[256,128]{1,0:T(8,128)(2,1)}) custom-call(bf16[256,2048]{1,0:T(8,128)(2,1)} %raw_ref.3, s32[2,128]{1,0:T(2,128)} %bitcast.90, s32[1,102]{1,0:T(1,128)} %bitcast.91, ...), custom_call_target="tpu_custom_call" | custom-call | tf_op jit(solution)/shard_map/prepare/pallas_call | solution.py:157
  4.7 2.7 %collective-permute-start.1 = (bf16[16,2304]{1,0:T(8,128)(2,1)S(1)}, bf16[16,2304]{1,0:T(8,128)(2,1)S(1)}, u32[]{:S(2)}, u32[]{:S(2)}) collective-permute-start(bf16[16,2304]{1,0:T(8,128)(2,1)S(1)} %get-tuple-element.185), channel_id=1, source_target_pairs={{0,2},{4,6},{2,0},{6,4},{1,3},{5,7},{3,1},{7,5},{8,10},{12,14},{10... | collective-permute-start | bytes 221192 | tf_op jit(solution)/shard_map/ppermute | solution.py:888
  8.1 8.8 %inner.1.inner_ref = bf16[224,2048]{1,0:T(8,128)(2,1)S(1)} custom-call(bf16[256,2048]{1,0:T(8,128)(2,1)S(1)} %copy-done, bf16[256,128]{1,0:T(8,128)(2,1)S(1)} %copy-done.1, bf16[256,128]{1,0:T(8,128)(2,1)S(1)} %get-tuple-element.191.left_ref, bf16[256,128]{1,0:T(8,128)(2,1)S(1)} %get-tuple-element.190.right_ref, bf16[11,768,256]{2,1,0:T(8,128)(2,1)S(1)} %bands.1.band_ref), custom_call_target="tpu_custom_call" | custom-call | flops 7751073792 | bytes 6291456 | tf_op jit(solution)/shard_map/inner/pallas_call | solution.py:433
  17.0 3.5 %edges.1 = (bf16[256,2048]{1,0:T(8,128)(2,1)}, bf16[520,128]{1,0:T(8,128)(2,1)S(1)}, bf16[520,128]{1,0:T(8,128)(2,1)S(1)}, bf16[520,128]{1,0:T(8,128)(2,1)S(1)}, bf16[520,128]{1,0:T(8,128)(2,1)S(1)}) custom-call(s32[8,128]{1,0:T(8,128)S(1)} %copy-done.2, s32[1,128]{1,0:T(1,128)S(1)} %get-tuple-element.273.own_ref, bf16[224,2048]{1,0:T(8,128)(2,1)S(1)} %inner.1.inner_ref, ...), custom_call_target="tpu_custom_call" | custom-call | flops 1107296256 | bytes 6291456 | tf_op jit(solution)/shard_map/edges/pallas_call | solution.py:577
  20.5 1.5 %collective-permute-start.3 = (bf16[520,128]{1,0:T(8,128)(2,1)S(1)}, bf16[520,128]{1,0:T(8,128)(2,1)S(1)}, u32[]{:S(2)}, u32[]{:S(2)}) collective-permute-start(bf16[520,128]{1,0:T(8,128)(2,1)S(1)} %get-tuple-element.96), channel_id=1, source_target_pairs={{0,8},{8,0},{16,24},{24,16},{1,9},{9,1},{17,25},{25,17},{2,10},{10... | collective-permute-start | bytes 399368 | tf_op jit(solution)/shard_map/ppermute | solution.py:645
  22.0 1.5 %collective-permute-start.4 = (bf16[520,128]{1,0:T(8,128)(2,1)S(1)}, bf16[520,128]{1,0:T(8,128)(2,1)S(1)}, u32[]{:S(2)}, u32[]{:S(2)}) collective-permute-start(bf16[520,128]{1,0:T(8,128)(2,1)S(1)} %get-tuple-element.97), channel_id=1, source_target_pairs={{0,16},{8,24},{16,0},{24,8},{1,17},{9,25},{17,1},{25,9},{2,18},{10... | collective-permute-start | bytes 399368 | tf_op jit(solution)/shard_map/ppermute | solution.py:645
  24.0 1.6 %pack.1.tiles_ref = bf16[96,32,128]{2,1,0:T(8,128)(2,1)S(1)} custom-call(s32[8,128]{1,0:T(8,128)S(1)} %copy-done.2, bf16[256,2048]{1,0:T(8,128)(2,1)} %get-tuple-element.271.signal_ref), custom_call_target="tpu_custom_call" | custom-call | flops 100000000 | bytes 3145728 | tf_op jit(solution)/shard_map/pack/pallas_call | solution.py:664
  26.5 3.7 %collective-permute-done.4.refs_2_ = bf16[520,128]{1,0:T(8,128)(2,1)S(1)} collective-permute-done((bf16[520,128]{1,0:T(8,128)(2,1)S(1)}, bf16[520,128]{1,0:T(8,128)(2,1)S(1)}, u32[]{:S(2)}, u32[]{:S(2)}) %collective-permute-start.4) | collective-permute-done | bytes 133152 | tf_op jit(solution)/shard_map/ppermute | solution.py:645
  30.3 4.2 %collective-permute-start.6 = (bf16[136,128]{1,0:T(8,128)(2,1)S(1)}, bf16[136,128]{1,0:T(8,128)(2,1)S(1)}, u32[]{:S(2)}, u32[]{:S(2)}) collective-permute-start(bf16[136,128]{1,0:T(8,128)(2,1)S(1)} %get-tuple-element.104), channel_id=1, source_target_pairs={{0,2},{2,0},{4,6},{6,4},{1,3},{3,1},{5,7},{7,5},{8,10},{10,8},{12,... | collective-permute-start | bytes 104456 | tf_op jit(solution)/shard_map/ppermute | solution.py:645
  34.5 2.4 %collective-permute-start.8 = (bf16[136,128]{1,0:T(8,128)(2,1)S(1)}, bf16[136,128]{1,0:T(8,128)(2,1)S(1)}, u32[]{:S(2)}, u32[]{:S(2)}) collective-permute-start(bf16[136,128]{1,0:T(8,128)(2,1)S(1)} %get-tuple-element.106), channel_id=1, source_target_pairs={{0,6},{2,4},{4,2},{6,0},{1,7},{3,5},{5,3},{7,1},{8,14},{10,12},{12... | collective-permute-start | bytes 104456 | tf_op jit(solution)/shard_map/ppermute | solution.py:645
  36.9 2.4 %collective-permute-done.7.refs_2_ = bf16[136,128]{1,0:T(8,128)(2,1)S(1)} collective-permute-done((bf16[136,128]{1,0:T(8,128)(2,1)S(1)}, bf16[136,128]{1,0:T(8,128)(2,1)S(1)}, u32[]{:S(2)}, u32[]{:S(2)}) %collective-permute-start.7) | collective-permute-done | bytes 34848 | tf_op jit(solution)/shard_map/ppermute | solution.py:645
  41.1 1.6 %collective-permute-start.10 = (bf16[6,32,128]{2,1,0:T(8,128)(2,1)S(1)}, bf16[6,32,128]{2,1,0:T(8,128)(2,1)S(1)}, u32[]{:S(2)}, u32[]{:S(2)}) collective-permute-start(bf16[6,32,128]{2,1,0:T(8,128)(2,1)S(1)} %get-tuple-element.111), channel_id=1, source_target_pairs={{0,16},{2,18},{4,20},{6,22},{8,24},{10,26},{12,28},{14,30},{16,0},... | collective-permute-start | bytes 147464 | tf_op jit(solution)/shard_map/ppermute | solution.py:645
  45.1 2.2 %collective-permute-start.13 = (bf16[6,32,128]{2,1,0:T(8,128)(2,1)S(1)}, bf16[6,32,128]{2,1,0:T(8,128)(2,1)S(1)}, u32[]{:S(2)}, u32[]{:S(2)}) collective-permute-start(bf16[6,32,128]{2,1,0:T(8,128)(2,1)S(1)} %get-tuple-element.114), channel_id=1, source_target_pairs={{0,10},{2,8},{4,14},{6,12},{8,2},{10,0},{12,6},{14,4},{16,26},{18,... | collective-permute-start | bytes 147464 | tf_op jit(solution)/shard_map/ppermute | solution.py:645
  48.6 2.3 %collective-permute-start.15 = (bf16[6,32,128]{2,1,0:T(8,128)(2,1)S(1)}, bf16[6,32,128]{2,1,0:T(8,128)(2,1)S(1)}, u32[]{:S(2)}, u32[]{:S(2)}) collective-permute-start(bf16[6,32,128]{2,1,0:T(8,128)(2,1)S(1)} %get-tuple-element.116), channel_id=1, source_target_pairs={{0,26},{2,24},{4,30},{6,28},{8,18},{10,16},{12,22},{14,20},{16,10}... | collective-permute-start | bytes 147464 | tf_op jit(solution)/shard_map/ppermute | solution.py:645
  50.9 1.5 %collective-permute-start.16 = (bf16[6,32,128]{2,1,0:T(8,128)(2,1)S(1)}, bf16[6,32,128]{2,1,0:T(8,128)(2,1)S(1)}, u32[]{:S(2)}, u32[]{:S(2)}) collective-permute-start(bf16[6,32,128]{2,1,0:T(8,128)(2,1)S(1)} %get-tuple-element.117), channel_id=1, source_target_pairs={{0,4},{2,6},{4,0},{6,2},{8,12},{10,14},{12,8},{14,10},{16,20},{18,... | collective-permute-start | bytes 147464 | tf_op jit(solution)/shard_map/ppermute | solution.py:645
  52.4 1.6 %collective-permute-start.17 = (bf16[6,32,128]{2,1,0:T(8,128)(2,1)S(1)}, bf16[6,32,128]{2,1,0:T(8,128)(2,1)S(1)}, u32[]{:S(2)}, u32[]{:S(2)}) collective-permute-start(bf16[6,32,128]{2,1,0:T(8,128)(2,1)S(1)} %get-tuple-element.118), channel_id=1, source_target_pairs={{0,12},{2,14},{4,8},{6,10},{8,4},{10,6},{12,0},{14,2},{16,28},{18,... | collective-permute-start | bytes 147464 | tf_op jit(solution)/shard_map/ppermute | solution.py:645
  54.0 2.2 %collective-permute-start.18 = (bf16[6,32,128]{2,1,0:T(8,128)(2,1)S(1)}, bf16[6,32,128]{2,1,0:T(8,128)(2,1)S(1)}, u32[]{:S(2)}, u32[]{:S(2)}) collective-permute-start(bf16[6,32,128]{2,1,0:T(8,128)(2,1)S(1)} %get-tuple-element.119), channel_id=1, source_target_pairs={{0,20},{2,22},{4,16},{6,18},{8,28},{10,30},{12,24},{14,26},{16,4},... | collective-permute-start | bytes 147464 | tf_op jit(solution)/shard_map/ppermute | solution.py:645
  56.3 2.3 %collective-permute-start.19 = (bf16[6,32,128]{2,1,0:T(8,128)(2,1)S(1)}, bf16[6,32,128]{2,1,0:T(8,128)(2,1)S(1)}, u32[]{:S(2)}, u32[]{:S(2)}) collective-permute-start(bf16[6,32,128]{2,1,0:T(8,128)(2,1)S(1)} %get-tuple-element.120), channel_id=1, source_target_pairs={{0,28},{2,30},{4,24},{6,26},{8,20},{10,22},{12,16},{14,18},{16,12}... | collective-permute-start | bytes 147464 | tf_op jit(solution)/shard_map/ppermute | solution.py:645
  58.6 2.4 %collective-permute-start.20 = (bf16[6,32,128]{2,1,0:T(8,128)(2,1)S(1)}, bf16[6,32,128]{2,1,0:T(8,128)(2,1)S(1)}, u32[]{:S(2)}, u32[]{:S(2)}) collective-permute-start(bf16[6,32,128]{2,1,0:T(8,128)(2,1)S(1)} %get-tuple-element.121), channel_id=1, source_target_pairs={{0,6},{2,4},{4,2},{6,0},{8,14},{10,12},{12,10},{14,8},{16,22},{18,... | collective-permute-start | bytes 147464 | tf_op jit(solution)/shard_map/ppermute | solution.py:645
  61.0 1.6 %collective-permute-start.21 = (bf16[6,32,128]{2,1,0:T(8,128)(2,1)S(1)}, bf16[6,32,128]{2,1,0:T(8,128)(2,1)S(1)}, u32[]{:S(2)}, u32[]{:S(2)}) collective-permute-start(bf16[6,32,128]{2,1,0:T(8,128)(2,1)S(1)} %get-tuple-element.122), channel_id=1, source_target_pairs={{0,14},{2,12},{4,10},{6,8},{8,6},{10,4},{12,2},{14,0},{16,30},{18,... | collective-permute-start | bytes 147464 | tf_op jit(solution)/shard_map/ppermute | solution.py:645
  62.6 3.4 %collective-permute-start.22 = (bf16[6,32,128]{2,1,0:T(8,128)(2,1)S(1)}, bf16[6,32,128]{2,1,0:T(8,128)(2,1)S(1)}, u32[]{:S(2)}, u32[]{:S(2)}) collective-permute-start(bf16[6,32,128]{2,1,0:T(8,128)(2,1)S(1)} %get-tuple-element.123), channel_id=1, source_target_pairs={{0,22},{2,20},{4,18},{6,16},{8,30},{10,28},{12,26},{14,24},{16,6},... | collective-permute-start | bytes 147464 | tf_op jit(solution)/shard_map/ppermute | solution.py:645
  66.0 2.0 %collective-permute-start.23 = (bf16[6,32,128]{2,1,0:T(8,128)(2,1)S(1)}, bf16[6,32,128]{2,1,0:T(8,128)(2,1)S(1)}, u32[]{:S(2)}, u32[]{:S(2)}) collective-permute-start(bf16[6,32,128]{2,1,0:T(8,128)(2,1)S(1)} %get-tuple-element.124), channel_id=1, source_target_pairs={{0,30},{2,28},{4,26},{6,24},{8,22},{10,20},{12,18},{14,16},{16,14}... | collective-permute-start | bytes 147464 | tf_op jit(solution)/shard_map/ppermute | solution.py:645
  71.7 2.0 %collective-permute-done.23.refs_15_ = bf16[6,32,128]{2,1,0:T(8,128)(2,1)S(1)} collective-permute-done((bf16[6,32,128]{2,1,0:T(8,128)(2,1)S(1)}, bf16[6,32,128]{2,1,0:T(8,128)(2,1)S(1)}, u32[]{:S(2)}, u32[]{:S(2)}) %collective-permute-start.23) | collective-permute-done | bytes 49184 | tf_op jit(solution)/shard_map/ppermute | solution.py:645
  73.7 2.6 %image.1 = f32[128,2048]{1,0:T(8,128)} custom-call(s32[8,128]{1,0:T(8,128)S(1)} %get-tuple-element.274.plan_ref, bf16[26,128,256]{2,1,0:T(8,128)(2,1)S(1)} %stage.1.staged_ref, bf16[6,32,128]{2,1,0:T(8,128)(2,1)S(1)} %get-tuple-element.109.refs_0_, bf16[6,32,128]{2,1,0:T(8,128)(2,1)S(1)} %collective-permute-done.9.refs_1_, ...), custom_call_target="tpu_custom_call" | custom-call | flops 100000000 | bytes 3145728 | tf_op jit(solution)/shard_map/image/pallas_call | solution.py:771
  (61 shorter events, 12.1 us)
Async XLA Ops:
  4.7 12.2 %collective-permute-start.1 = (bf16[16,2304]{1,0:T(8,128)(2,1)S(1)}, bf16[16,2304]{1,0:T(8,128)(2,1)S(1)}, u32[]{:S(2)}, u32[]{:S(2)}) collective-permute-start(bf16[16,2304]{1,0:T(8,128)(2,1)S(1)} %get-tuple-element.185), channel_id=1, source_target_pairs={{0,2},{4,6},{2,0},{6,4},{1,3},{5,7},{3,1},{7,5},{8,10},{12,14},{10... | collective-permute-start | bytes 221192 | tf_op jit(solution)/shard_map/ppermute | solution.py:888
  7.4 9.6 %collective-permute-start.2 = (bf16[16,2304]{1,0:T(8,128)(2,1)S(1)}, bf16[16,2304]{1,0:T(8,128)(2,1)S(1)}, u32[]{:S(2)}, u32[]{:S(2)}) collective-permute-start(bf16[16,2304]{1,0:T(8,128)(2,1)S(1)} %get-tuple-element.184), channel_id=1, source_target_pairs={{2,4},{4,2},{3,5},{5,3},{10,12},{12,10},{11,13},{13,11},{18,20},{2... | collective-permute-start | bytes 221192 | tf_op jit(solution)/shard_map/ppermute | solution.py:888
  20.5 6.0 %collective-permute-start.3 = (bf16[520,128]{1,0:T(8,128)(2,1)S(1)}, bf16[520,128]{1,0:T(8,128)(2,1)S(1)}, u32[]{:S(2)}, u32[]{:S(2)}) collective-permute-start(bf16[520,128]{1,0:T(8,128)(2,1)S(1)} %get-tuple-element.96), channel_id=1, source_target_pairs={{0,8},{8,0},{16,24},{24,16},{1,9},{9,1},{17,25},{25,17},{2,10},{10... | collective-permute-start | bytes 399368 | tf_op jit(solution)/shard_map/ppermute | solution.py:645
  22.0 8.2 %collective-permute-start.4 = (bf16[520,128]{1,0:T(8,128)(2,1)S(1)}, bf16[520,128]{1,0:T(8,128)(2,1)S(1)}, u32[]{:S(2)}, u32[]{:S(2)}) collective-permute-start(bf16[520,128]{1,0:T(8,128)(2,1)S(1)} %get-tuple-element.97), channel_id=1, source_target_pairs={{0,16},{8,24},{16,0},{24,8},{1,17},{9,25},{17,1},{25,9},{2,18},{10... | collective-permute-start | bytes 399368 | tf_op jit(solution)/shard_map/ppermute | solution.py:645
  23.5 6.7 %collective-permute-start.5 = (bf16[520,128]{1,0:T(8,128)(2,1)S(1)}, bf16[520,128]{1,0:T(8,128)(2,1)S(1)}, u32[]{:S(2)}, u32[]{:S(2)}) collective-permute-start(bf16[520,128]{1,0:T(8,128)(2,1)S(1)} %get-tuple-element.98), channel_id=1, source_target_pairs={{0,24},{8,16},{16,8},{24,0},{1,25},{9,17},{17,9},{25,1},{2,26},{10... | collective-permute-start | bytes 399368 | tf_op jit(solution)/shard_map/ppermute | solution.py:645
  30.3 6.6 %collective-permute-start.6 = (bf16[136,128]{1,0:T(8,128)(2,1)S(1)}, bf16[136,128]{1,0:T(8,128)(2,1)S(1)}, u32[]{:S(2)}, u32[]{:S(2)}) collective-permute-start(bf16[136,128]{1,0:T(8,128)(2,1)S(1)} %get-tuple-element.104), channel_id=1, source_target_pairs={{0,2},{2,0},{4,6},{6,4},{1,3},{3,1},{5,7},{7,5},{8,10},{10,8},{12,... | collective-permute-start | bytes 104456 | tf_op jit(solution)/shard_map/ppermute | solution.py:645
  34.5 4.8 %collective-permute-start.7 = (bf16[136,128]{1,0:T(8,128)(2,1)S(1)}, bf16[136,128]{1,0:T(8,128)(2,1)S(1)}, u32[]{:S(2)}, u32[]{:S(2)}) collective-permute-start(bf16[136,128]{1,0:T(8,128)(2,1)S(1)} %get-tuple-element.105), channel_id=1, source_target_pairs={{0,4},{2,6},{4,0},{6,2},{1,5},{3,7},{5,1},{7,3},{8,12},{10,14},{12... | collective-permute-start | bytes 104456 | tf_op jit(solution)/shard_map/ppermute | solution.py:645
  34.5 5.7 %collective-permute-start.8 = (bf16[136,128]{1,0:T(8,128)(2,1)S(1)}, bf16[136,128]{1,0:T(8,128)(2,1)S(1)}, u32[]{:S(2)}, u32[]{:S(2)}) collective-permute-start(bf16[136,128]{1,0:T(8,128)(2,1)S(1)} %get-tuple-element.106), channel_id=1, source_target_pairs={{0,6},{2,4},{4,2},{6,0},{1,7},{3,5},{5,3},{7,1},{8,14},{10,12},{12... | collective-permute-start | bytes 104456 | tf_op jit(solution)/shard_map/ppermute | solution.py:645
  41.1 7.5 %collective-permute-start.10 = (bf16[6,32,128]{2,1,0:T(8,128)(2,1)S(1)}, bf16[6,32,128]{2,1,0:T(8,128)(2,1)S(1)}, u32[]{:S(2)}, u32[]{:S(2)}) collective-permute-start(bf16[6,32,128]{2,1,0:T(8,128)(2,1)S(1)} %get-tuple-element.111), channel_id=1, source_target_pairs={{0,16},{2,18},{4,20},{6,22},{8,24},{10,26},{12,28},{14,30},{16,0},... | collective-permute-start | bytes 147464 | tf_op jit(solution)/shard_map/ppermute | solution.py:645
  42.7 8.2 %collective-permute-start.11 = (bf16[6,32,128]{2,1,0:T(8,128)(2,1)S(1)}, bf16[6,32,128]{2,1,0:T(8,128)(2,1)S(1)}, u32[]{:S(2)}, u32[]{:S(2)}) collective-permute-start(bf16[6,32,128]{2,1,0:T(8,128)(2,1)S(1)} %get-tuple-element.112), channel_id=1, source_target_pairs={{0,24},{2,26},{4,28},{6,30},{8,16},{10,18},{12,20},{14,22},{16,8},... | collective-permute-start | bytes 147464 | tf_op jit(solution)/shard_map/ppermute | solution.py:645
  45.0 7.4 %collective-permute-start.12 = (bf16[6,32,128]{2,1,0:T(8,128)(2,1)S(1)}, bf16[6,32,128]{2,1,0:T(8,128)(2,1)S(1)}, u32[]{:S(2)}, u32[]{:S(2)}) collective-permute-start(bf16[6,32,128]{2,1,0:T(8,128)(2,1)S(1)} %get-tuple-element.113), channel_id=1, source_target_pairs={{0,2},{2,0},{4,6},{6,4},{8,10},{10,8},{12,14},{14,12},{16,18},{18,... | collective-permute-start | bytes 147464 | tf_op jit(solution)/shard_map/ppermute | solution.py:645
  45.1 2.2 %collective-permute-start.24 = (s32[1,1]{1,0:T(1,128)}, s32[1,1]{1,0:T(1,128)}, u32[]{:S(2)}, u32[]{:S(2)}) collective-permute-start(s32[1,1]{1,0:T(1,128)} %slice.28), channel_id=1, source_target_pairs={{0,1},{1,0},{2,3},{3,2},{4,5},{5,4},{6,7},{7,6},{8,9},{9,8},{10,11... | collective-permute-start | bytes 20 | tf_op jit(solution)/shard_map/ppermute | solution.py:281
  45.1 9.0 %collective-permute-start.13 = (bf16[6,32,128]{2,1,0:T(8,128)(2,1)S(1)}, bf16[6,32,128]{2,1,0:T(8,128)(2,1)S(1)}, u32[]{:S(2)}, u32[]{:S(2)}) collective-permute-start(bf16[6,32,128]{2,1,0:T(8,128)(2,1)S(1)} %get-tuple-element.114), channel_id=1, source_target_pairs={{0,10},{2,8},{4,14},{6,12},{8,2},{10,0},{12,6},{14,4},{16,26},{18,... | collective-permute-start | bytes 147464 | tf_op jit(solution)/shard_map/ppermute | solution.py:645
  47.3 9.0 %collective-permute-start.14 = (bf16[6,32,128]{2,1,0:T(8,128)(2,1)S(1)}, bf16[6,32,128]{2,1,0:T(8,128)(2,1)S(1)}, u32[]{:S(2)}, u32[]{:S(2)}) collective-permute-start(bf16[6,32,128]{2,1,0:T(8,128)(2,1)S(1)} %get-tuple-element.115), channel_id=1, source_target_pairs={{0,18},{2,16},{4,22},{6,20},{8,26},{10,24},{12,30},{14,28},{16,2},... | collective-permute-start | bytes 147464 | tf_op jit(solution)/shard_map/ppermute | solution.py:645
  48.6 10.0 %collective-permute-start.15 = (bf16[6,32,128]{2,1,0:T(8,128)(2,1)S(1)}, bf16[6,32,128]{2,1,0:T(8,128)(2,1)S(1)}, u32[]{:S(2)}, u32[]{:S(2)}) collective-permute-start(bf16[6,32,128]{2,1,0:T(8,128)(2,1)S(1)} %get-tuple-element.116), channel_id=1, source_target_pairs={{0,26},{2,24},{4,30},{6,28},{8,18},{10,16},{12,22},{14,20},{16,10}... | collective-permute-start | bytes 147464 | tf_op jit(solution)/shard_map/ppermute | solution.py:645
  50.9 10.1 %collective-permute-start.16 = (bf16[6,32,128]{2,1,0:T(8,128)(2,1)S(1)}, bf16[6,32,128]{2,1,0:T(8,128)(2,1)S(1)}, u32[]{:S(2)}, u32[]{:S(2)}) collective-permute-start(bf16[6,32,128]{2,1,0:T(8,128)(2,1)S(1)} %get-tuple-element.117), channel_id=1, source_target_pairs={{0,4},{2,6},{4,0},{6,2},{8,12},{10,14},{12,8},{14,10},{16,20},{18,... | collective-permute-start | bytes 147464 | tf_op jit(solution)/shard_map/ppermute | solution.py:645
  52.4 10.2 %collective-permute-start.17 = (bf16[6,32,128]{2,1,0:T(8,128)(2,1)S(1)}, bf16[6,32,128]{2,1,0:T(8,128)(2,1)S(1)}, u32[]{:S(2)}, u32[]{:S(2)}) collective-permute-start(bf16[6,32,128]{2,1,0:T(8,128)(2,1)S(1)} %get-tuple-element.118), channel_id=1, source_target_pairs={{0,12},{2,14},{4,8},{6,10},{8,4},{10,6},{12,0},{14,2},{16,28},{18,... | collective-permute-start | bytes 147464 | tf_op jit(solution)/shard_map/ppermute | solution.py:645
  54.0 12.0 %collective-permute-start.18 = (bf16[6,32,128]{2,1,0:T(8,128)(2,1)S(1)}, bf16[6,32,128]{2,1,0:T(8,128)(2,1)S(1)}, u32[]{:S(2)}, u32[]{:S(2)}) collective-permute-start(bf16[6,32,128]{2,1,0:T(8,128)(2,1)S(1)} %get-tuple-element.119), channel_id=1, source_target_pairs={{0,20},{2,22},{4,16},{6,18},{8,28},{10,30},{12,24},{14,26},{16,4},... | collective-permute-start | bytes 147464 | tf_op jit(solution)/shard_map/ppermute | solution.py:645
  56.3 11.7 %collective-permute-start.19 = (bf16[6,32,128]{2,1,0:T(8,128)(2,1)S(1)}, bf16[6,32,128]{2,1,0:T(8,128)(2,1)S(1)}, u32[]{:S(2)}, u32[]{:S(2)}) collective-permute-start(bf16[6,32,128]{2,1,0:T(8,128)(2,1)S(1)} %get-tuple-element.120), channel_id=1, source_target_pairs={{0,28},{2,30},{4,24},{6,26},{8,20},{10,22},{12,16},{14,18},{16,12}... | collective-permute-start | bytes 147464 | tf_op jit(solution)/shard_map/ppermute | solution.py:645
  58.6 13.1 %collective-permute-start.20 = (bf16[6,32,128]{2,1,0:T(8,128)(2,1)S(1)}, bf16[6,32,128]{2,1,0:T(8,128)(2,1)S(1)}, u32[]{:S(2)}, u32[]{:S(2)}) collective-permute-start(bf16[6,32,128]{2,1,0:T(8,128)(2,1)S(1)} %get-tuple-element.121), channel_id=1, source_target_pairs={{0,6},{2,4},{4,2},{6,0},{8,14},{10,12},{12,10},{14,8},{16,22},{18,... | collective-permute-start | bytes 147464 | tf_op jit(solution)/shard_map/ppermute | solution.py:645
  61.0 10.7 %collective-permute-start.21 = (bf16[6,32,128]{2,1,0:T(8,128)(2,1)S(1)}, bf16[6,32,128]{2,1,0:T(8,128)(2,1)S(1)}, u32[]{:S(2)}, u32[]{:S(2)}) collective-permute-start(bf16[6,32,128]{2,1,0:T(8,128)(2,1)S(1)} %get-tuple-element.122), channel_id=1, source_target_pairs={{0,14},{2,12},{4,10},{6,8},{8,6},{10,4},{12,2},{14,0},{16,30},{18,... | collective-permute-start | bytes 147464 | tf_op jit(solution)/shard_map/ppermute | solution.py:645
  62.6 9.1 %collective-permute-start.22 = (bf16[6,32,128]{2,1,0:T(8,128)(2,1)S(1)}, bf16[6,32,128]{2,1,0:T(8,128)(2,1)S(1)}, u32[]{:S(2)}, u32[]{:S(2)}) collective-permute-start(bf16[6,32,128]{2,1,0:T(8,128)(2,1)S(1)} %get-tuple-element.123), channel_id=1, source_target_pairs={{0,22},{2,20},{4,18},{6,16},{8,30},{10,28},{12,26},{14,24},{16,6},... | collective-permute-start | bytes 147464 | tf_op jit(solution)/shard_map/ppermute | solution.py:645
  66.0 7.7 %collective-permute-start.23 = (bf16[6,32,128]{2,1,0:T(8,128)(2,1)S(1)}, bf16[6,32,128]{2,1,0:T(8,128)(2,1)S(1)}, u32[]{:S(2)}, u32[]{:S(2)}) collective-permute-start(bf16[6,32,128]{2,1,0:T(8,128)(2,1)S(1)} %get-tuple-element.124), channel_id=1, source_target_pairs={{0,30},{2,28},{4,26},{6,24},{8,22},{10,20},{12,18},{14,16},{16,14}... | collective-permute-start | bytes 147464 | tf_op jit(solution)/shard_map/ppermute | solution.py:645
  68.0 5.7 %collective-permute-start.9 = (bf16[6,32,128]{2,1,0:T(8,128)(2,1)S(1)}, bf16[6,32,128]{2,1,0:T(8,128)(2,1)S(1)}, u32[]{:S(2)}, u32[]{:S(2)}) collective-permute-start(bf16[6,32,128]{2,1,0:T(8,128)(2,1)S(1)} %get-tuple-element.110), channel_id=1, source_target_pairs={{0,8},{2,10},{4,12},{6,14},{8,0},{10,2},{12,4},{14,6},{16,24},{18,... | collective-permute-start | bytes 147464 | tf_op jit(solution)/shard_map/ppermute | solution.py:645
  (10 other events, 136.6 us)

commit v3 on v1

--- a/solution.py
+++ b/solution.py
@@ -427,7 +427,7 @@
     pairs = (wires - 2 * PAD) // 2
     chunks = []
     while sum(chunks) < pairs:
-        chunks.append(min(32 if chunks else 16, pairs - sum(chunks)))
+        chunks.append(min(32 if chunks else 24, pairs - sum(chunks)))
     flops = 2 * blocks * pairs * reach * 6 * TB * 2 * TB
     return pl.pallas_call(
         functools.partial(inner_kernel, tuple(chunks)),
@@ -435,9 +435,9 @@
         in_specs=[vmem()] * 5,
         out_specs=vmem(),
         scratch_shapes=[
-            pltpu.VMEM((wires * pitch, TB), jnp.float32),
+            pltpu.VMEM(((wires + 1) * pitch, TB), jnp.float32),
             pltpu.VMEM((pairs + reach - 1, blocks, 6 * TB), jnp.bfloat16),
-            pltpu.VMEM((2, 2 * max(chunks) * blocks, TB), jnp.float32),
+            pltpu.VMEM((2, (2 * max(chunks) + 1) * blocks, TB), jnp.float32),
         ],
         cost_estimate=pl.CostEstimate(flops=flops, bytes_accessed=6 * MIB, transcendentals=0),
         compiler_params=pltpu.CompilerParams(vmem_limit_bytes=28 * MIB),
@@ -583,9 +583,9 @@
         out_specs=(vmem(),) * (1 + planes),
         scratch_shapes=[
             pltpu.VMEM((planes, height, TB), jnp.bfloat16),
-            pltpu.VMEM((2, 3 * PAD * pitch, TB), jnp.float32),
+            pltpu.VMEM((2, (3 * PAD + 1) * pitch, TB), jnp.float32),
             pltpu.VMEM((2, PAD // 2 + reach - 1, blocks, 6 * TB), jnp.bfloat16),
-            pltpu.VMEM((2, PAD * blocks, TB), jnp.float32),
+            pltpu.VMEM((2, (PAD + 1) * blocks, TB), jnp.float32),
             pltpu.VMEM((cells, wires), jnp.bfloat16),
         ],
         cost_estimate=pl.CostEstimate(flops=flops, bytes_accessed=6 * MIB, transcendentals=0),

time: 66.1 us -> 66.2 us (level)
  no operation moved by 1% of the time
where the time goes in v3:
time: 66.2 us; the launch traced here: 65.8 us
  Pallas kernels  20.6 us (31%)
  waiting for transfers between devices  18.9 us (29%)
  starting transfers between devices  18.8 us (28%)
  between operations  3.98 us (6%)
  local copies, waits for them, and re-layouts  3.45 us (5%)
    all_to_all x1, waiting for transfers between devices, exchange(): return lax.all_to_all(array, axes, split_axis=0, concat_axis=0, tiled=True)  13.6 us
    ppermute x6, starting transfers between devices, swap_all(): got.append(lax.ppermute(parts[step], axis, pairs))  10.2 us
    pallas_call x1, Pallas kernels, convolve_inner(): pl.pallas_call(functools.partial(inner_kernel, tuple(chunks)), out_shape=...  8.7 us
    ppermute x6, waiting for transfers between devices, swap_all(): got.append(lax.ppermute(parts[step], axis, pairs))  5.24 us
    all_to_all x1, starting transfers between devices, exchange(): return lax.all_to_all(array, axes, split_axis=0, concat_axis=0, tiled=True)  4.81 us
    ppermute x2, starting transfers between devices, wire_halo(): got.append(lax.ppermute(rows, 'wire', pairs + [(j, i) for i, j in pairs]))  3.32 us
    pallas_call x1, Pallas kernels, make_image(): pl.pallas_call(functools.partial(image_kernel, owner_total, share), out_s...  2.78 us
    pallas_call x1, Pallas kernels, convolve_edges(): pl.pallas_call(functools.partial(edge_kernel, planes), out_shape=(jax.Sha...  2.65 us
  transfers between devices with their start and end apart: 11, of which 4 were waited for; matrix products, arithmetic and copies ran while one was open for 3% of the time, Pallas kernels for 20%

profile of v3, /device:TPU:0, one launch (start us, length us, event | category | flops | bytes accessed | tf_op | source)
XLA Modules:
  0.0 65.8 jit_solution(17110836096285314543)
XLA Ops:
  0.6 1.9 %prepare.1 = (bf16[256,128]{1,0:T(8,128)(2,1)}, bf16[16,2048]{1,0:T(8,128)(2,1)}, bf16[16,2048]{1,0:T(8,128)(2,1)}, s32[1,128]{1,0:T(1,128)S(1)}, s32[8,128]{1,0:T(8,128)}, /*index=5*/bf16[256,128]{1,0:T(8,128)(2,1)}) custom-call(bf16[256,2048]{1,0:T(8,128)(2,1)} %raw_ref.3, s32[2,128]{1,0:T(2,128)} %bitcast.97, s32[1,102]{1,0:T(1,128)} %bitcast.98, ...), custom_call_target="tpu_custom_call" | custom-call | tf_op jit(solution)/shard_map/prepare/pallas_call | solution.py:156
  3.1 0.7 %copy-done.3 = bf16[1,21,256]{2,1,0:T(8,128)(2,1)S(1)} copy-done((bf16[1,21,256]{2,1,0:T(8,128)(2,1)S(1)}, bf16[1,21,256]{2,1,0:T(8,128)(2,1)}, u32[]{:S(2)}) %copy-start.3) | copy-done | bytes 10776
  3.8 0.6 bands.1.band_ref
  4.7 2.7 %collective-permute-start.1 = (bf16[16,2304]{1,0:T(8,128)(2,1)S(1)}, bf16[16,2304]{1,0:T(8,128)(2,1)S(1)}, u32[]{:S(2)}, u32[]{:S(2)}) collective-permute-start(bf16[16,2304]{1,0:T(8,128)(2,1)S(1)} %get-tuple-element.153), channel_id=1, source_target_pairs={{0,2},{4,6},{2,0},{6,4},{1,3},{5,7},{3,1},{7,5},{8,10},{12,14},{10... | collective-permute-start | bytes 221192 | tf_op jit(solution)/shard_map/ppermute | solution.py:849
  7.4 0.7 collective-permute-start.2
  8.1 8.7 %inner.1.inner_ref = bf16[224,2048]{1,0:T(8,128)(2,1)S(1)} custom-call(bf16[256,2048]{1,0:T(8,128)(2,1)S(1)} %copy-done, bf16[256,128]{1,0:T(8,128)(2,1)S(1)} %copy-done.1, bf16[256,128]{1,0:T(8,128)(2,1)S(1)} %get-tuple-element.159.left_ref, bf16[256,128]{1,0:T(8,128)(2,1)S(1)} %get-tuple-element.158.right_ref, bf16[11,768,256]{2,1,0:T(8,128)(2,1)S(1)} %bands.1.band_ref), custom_call_target="tpu_custom_call" | custom-call | flops 7751073792 | bytes 6291456 | tf_op jit(solution)/shard_map/inner/pallas_call | solution.py:432
  16.9 2.6 %edges.1 = (bf16[256,2048]{1,0:T(8,128)(2,1)S(1)}, bf16[520,128]{1,0:T(8,128)(2,1)S(1)}, bf16[520,128]{1,0:T(8,128)(2,1)S(1)}, bf16[520,128]{1,0:T(8,128)(2,1)S(1)}, bf16[520,128]{1,0:T(8,128)(2,1)S(1)}) custom-call(s32[8,128]{1,0:T(8,128)S(1)} %copy-done.2, s32[1,128]{1,0:T(1,128)S(1)} %get-tuple-element.241.own_ref, bf16[224,2048]{1,0:T(8,128)(2,1)S(1)} %inner.1.inner_ref, ...), custom_call_target="tpu_custom_call" | custom-call | flops 1107296256 | bytes 6291456 | tf_op jit(solution)/shard_map/edges/pallas_call | solution.py:576
  19.5 1.6 %collective-permute-start.3 = (bf16[520,128]{1,0:T(8,128)(2,1)S(1)}, bf16[520,128]{1,0:T(8,128)(2,1)S(1)}, u32[]{:S(2)}, u32[]{:S(2)}) collective-permute-start(bf16[520,128]{1,0:T(8,128)(2,1)S(1)} %get-tuple-element.80), channel_id=1, source_target_pairs={{0,8},{8,0},{16,24},{24,16},{1,9},{9,1},{17,25},{25,17},{2,10},{10... | collective-permute-start | bytes 399368 | tf_op jit(solution)/shard_map/ppermute | solution.py:640
  21.1 1.5 %collective-permute-start.4 = (bf16[520,128]{1,0:T(8,128)(2,1)S(1)}, bf16[520,128]{1,0:T(8,128)(2,1)S(1)}, u32[]{:S(2)}, u32[]{:S(2)}) collective-permute-start(bf16[520,128]{1,0:T(8,128)(2,1)S(1)} %get-tuple-element.81), channel_id=1, source_target_pairs={{0,16},{8,24},{16,0},{24,8},{1,17},{9,25},{17,1},{25,9},{2,18},{10... | collective-permute-start | bytes 399368 | tf_op jit(solution)/shard_map/ppermute | solution.py:640
  23.1 1.8 %pack.1 = bf16[96,32,128]{2,1,0:T(8,128)(2,1)} custom-call(s32[8,128]{1,0:T(8,128)S(1)} %copy-done.2, bf16[256,2048]{1,0:T(8,128)(2,1)S(1)} %get-tuple-element.239.signal_ref), custom_call_target="tpu_custom_call" | custom-call | flops 100000000 | bytes 3145728 | tf_op jit(solution)/shard_map/pack/pallas_call | solution.py:659
  24.9 0.7 %collective-permute-done.3.refs_1_ = bf16[520,128]{1,0:T(8,128)(2,1)S(1)} collective-permute-done((bf16[520,128]{1,0:T(8,128)(2,1)S(1)}, bf16[520,128]{1,0:T(8,128)(2,1)S(1)}, u32[]{:S(2)}, u32[]{:S(2)}) %collective-permute-start.3) | collective-permute-done | bytes 133152 | tf_op jit(solution)/shard_map/ppermute | solution.py:640
  25.6 3.7 %collective-permute-done.4.refs_2_ = bf16[520,128]{1,0:T(8,128)(2,1)S(1)} collective-permute-done((bf16[520,128]{1,0:T(8,128)(2,1)S(1)}, bf16[520,128]{1,0:T(8,128)(2,1)S(1)}, u32[]{:S(2)}, u32[]{:S(2)}) %collective-permute-start.4) | collective-permute-done | bytes 133152 | tf_op jit(solution)/shard_map/ppermute | solution.py:640
  29.4 4.2 %collective-permute-start.6 = (bf16[136,128]{1,0:T(8,128)(2,1)S(1)}, bf16[136,128]{1,0:T(8,128)(2,1)S(1)}, u32[]{:S(2)}, u32[]{:S(2)}) collective-permute-start(bf16[136,128]{1,0:T(8,128)(2,1)S(1)} %get-tuple-element.88), channel_id=1, source_target_pairs={{0,2},{2,0},{4,6},{6,4},{1,3},{3,1},{5,7},{7,5},{8,10},{10,8},{12,... | collective-permute-start | bytes 104456 | tf_op jit(solution)/shard_map/ppermute | solution.py:640
  33.6 2.4 %collective-permute-start.8 = (bf16[136,128]{1,0:T(8,128)(2,1)S(1)}, bf16[136,128]{1,0:T(8,128)(2,1)S(1)}, u32[]{:S(2)}, u32[]{:S(2)}) collective-permute-start(bf16[136,128]{1,0:T(8,128)(2,1)S(1)} %get-tuple-element.90), channel_id=1, source_target_pairs={{0,6},{2,4},{4,2},{6,0},{1,7},{3,5},{5,3},{7,1},{8,14},{10,12},{12... | collective-permute-start | bytes 104456 | tf_op jit(solution)/shard_map/ppermute | solution.py:640
  36.0 0.6 slice.47
  38.5 0.8 %collective-permute-done.8.refs_3_ = bf16[136,128]{1,0:T(8,128)(2,1)S(1)} collective-permute-done((bf16[136,128]{1,0:T(8,128)(2,1)S(1)}, bf16[136,128]{1,0:T(8,128)(2,1)S(1)}, u32[]{:S(2)}, u32[]{:S(2)}) %collective-permute-start.8) | collective-permute-done | bytes 34848 | tf_op jit(solution)/shard_map/ppermute | solution.py:640
  39.3 0.6 constant_dynamic-update-slice_fusion
  40.0 4.8 %all-to-all-start.1 = ((bf16[16,6,32,128]{3,2,1,0:T(8,128)(2,1)}), bf16[16,6,32,128]{3,2,1,0:T(8,128)(2,1)S(1)}, u32[]{:S(2)}, u32[]{:S(2)}) async-start(bf16[16,6,32,128]{3,2,1,0:T(8,128)(2,1)} %constant_dynamic-update-slice_fusion), calls=%async_computation.1 | async-start | bytes 1572864 | tf_op jit(solution)/shard_map/all_to_all | solution.py:854
  44.8 0.6 receive_plan.1
  45.4 0.6 slice.48
  46.0 0.7 %copy.29 = s32[16,128]{0,1:T(8,128)} copy(s32[16,128]{1,0:T(8,128)S(1)} %get-tuple-element.123) | data formatting | bytes 16384 | tf_op jit(solution)/shard_map/while | solution.py:901
  46.7 1.4 %stage.1.staged_ref = bf16[26,128,256]{2,1,0:T(8,128)(2,1)S(1)} custom-call(s32[8,128]{1,0:T(8,128)S(1)} %get-tuple-element.242.plan_ref, bf16[128,32,128]{2,1,0:T(8,128)(2,1)S(1)} %copy-done.4), custom_call_target="tpu_custom_call" | custom-call | flops 100000000 | bytes 3145728 | tf_op jit(solution)/shard_map/stage/pallas_call | solution.py:683
  49.4 13.6 %all-to-all-done.1 = bf16[16,6,32,128]{3,2,1,0:T(8,128)(2,1)S(1)} async-done(((bf16[16,6,32,128]{3,2,1,0:T(8,128)(2,1)}), bf16[16,6,32,128]{3,2,1,0:T(8,128)(2,1)S(1)}, u32[]{:S(2)}, u32[]{:S(2)}) %all-to-all-start.1) | async-done | bytes 786464 | tf_op jit(solution)/shard_map/all_to_all | solution.py:854
  63.0 2.8 %image.1 = f32[128,2048]{1,0:T(8,128)} custom-call(s32[8,128]{1,0:T(8,128)S(1)} %get-tuple-element.242.plan_ref, bf16[96,32,128]{2,1,0:T(8,128)(2,1)S(1)} %bitcast.89, bf16[26,128,256]{2,1,0:T(8,128)(2,1)S(1)} %stage.1.staged_ref), custom_call_target="tpu_custom_call" | custom-call | flops 100000000 | bytes 3145728 | tf_op jit(solution)/shard_map/image/pallas_call | solution.py:732
  (37 shorter events, 1.4 us)
Async XLA Ops:
  0.6 7.4 %copy-start = (bf16[256,2048]{1,0:T(8,128)(2,1)S(1)}, bf16[256,2048]{1,0:T(8,128)(2,1)}, u32[]{:S(2)}) copy-start(bf16[256,2048]{1,0:T(8,128)(2,1)} %raw_ref.3) | copy-start | bytes 3145732
  2.6 5.5 %copy-start.1 = (bf16[256,128]{1,0:T(8,128)(2,1)S(1)}, bf16[256,128]{1,0:T(8,128)(2,1)}, u32[]{:S(2)}) copy-start(bf16[256,128]{1,0:T(8,128)(2,1)} %get-tuple-element.74.mask_ref) | copy-start | bytes 196612
  2.6 1.9 %collective-permute-start = (bf16[256,128]{1,0:T(8,128)(2,1)}, bf16[256,128]{1,0:T(8,128)(2,1)S(1)}, u32[]{:S(2)}, u32[]{:S(2)}) collective-permute-start(bf16[256,128]{1,0:T(8,128)(2,1)} %get-tuple-element.75), channel_id=1, source_target_pairs={{0,1},{1,0},{2,3},{3,2},{4,5},{5,4},{6,7},{7,6},{8,9},{9,8},{10,11... | collective-permute-start | bytes 196616 | tf_op jit(solution)/shard_map/ppermute | solution.py:833
  3.1 0.7 %copy-start.3 = (bf16[1,21,256]{2,1,0:T(8,128)(2,1)S(1)}, bf16[1,21,256]{2,1,0:T(8,128)(2,1)}, u32[]{:S(2)}) copy-start(bf16[1,21,256]{2,1,0:T(8,128)(2,1)} %param.10) | copy-start | bytes 32260
  3.8 0.8 %copy-start.7 = (bf16[16,2048]{1,0:T(8,128)(2,1)S(1)}, bf16[16,2048]{1,0:T(8,128)(2,1)}, u32[]{:S(2)}) copy-start(bf16[16,2048]{1,0:T(8,128)(2,1)} %get-tuple-element.76) | copy-start | bytes 196612
  3.8 0.9 %copy-start.8 = (bf16[16,2048]{1,0:T(8,128)(2,1)S(1)}, bf16[16,2048]{1,0:T(8,128)(2,1)}, u32[]{:S(2)}) copy-start(bf16[16,2048]{1,0:T(8,128)(2,1)} %get-tuple-element.77) | copy-start | bytes 196612
  4.7 12.1 %collective-permute-start.1 = (bf16[16,2304]{1,0:T(8,128)(2,1)S(1)}, bf16[16,2304]{1,0:T(8,128)(2,1)S(1)}, u32[]{:S(2)}, u32[]{:S(2)}) collective-permute-start(bf16[16,2304]{1,0:T(8,128)(2,1)S(1)} %get-tuple-element.153), channel_id=1, source_target_pairs={{0,2},{4,6},{2,0},{6,4},{1,3},{5,7},{3,1},{7,5},{8,10},{12,14},{10... | collective-permute-start | bytes 221192 | tf_op jit(solution)/shard_map/ppermute | solution.py:849
  7.4 9.4 %collective-permute-start.2 = (bf16[16,2304]{1,0:T(8,128)(2,1)S(1)}, bf16[16,2304]{1,0:T(8,128)(2,1)S(1)}, u32[]{:S(2)}, u32[]{:S(2)}) collective-permute-start(bf16[16,2304]{1,0:T(8,128)(2,1)S(1)} %get-tuple-element.152), channel_id=1, source_target_pairs={{2,4},{4,2},{3,5},{5,3},{10,12},{12,10},{11,13},{13,11},{18,20},{2... | collective-permute-start | bytes 221192 | tf_op jit(solution)/shard_map/ppermute | solution.py:849
  8.1 8.8 %copy-start.2 = (s32[8,128]{1,0:T(8,128)S(1)}, s32[8,128]{1,0:T(8,128)}, u32[]{:S(2)}) copy-start(s32[8,128]{1,0:T(8,128)} %get-tuple-element.72.plan_ref) | copy-start | bytes 12292
  8.1 8.8 %copy-start.4 = (bf16[128,32,128]{2,1,0:T(8,128)(2,1)S(1)}, bf16[128,32,128]{2,1,0:T(8,128)(2,1)}, u32[]{:S(2)}) copy-start(bf16[128,32,128]{2,1,0:T(8,128)(2,1)} %geo_ref.3) | copy-start | bytes 3145732
  19.5 20.4 %copy-start.5 = (bf16[256,2048]{1,0:T(8,128)(2,1)}, bf16[256,2048]{1,0:T(8,128)(2,1)S(1)}, u32[]{:S(2)}) copy-start(bf16[256,2048]{1,0:T(8,128)(2,1)S(1)} %get-tuple-element.239.signal_ref) | copy-start | bytes 3145732
  19.5 6.1 %collective-permute-start.3 = (bf16[520,128]{1,0:T(8,128)(2,1)S(1)}, bf16[520,128]{1,0:T(8,128)(2,1)S(1)}, u32[]{:S(2)}, u32[]{:S(2)}) collective-permute-start(bf16[520,128]{1,0:T(8,128)(2,1)S(1)} %get-tuple-element.80), channel_id=1, source_target_pairs={{0,8},{8,0},{16,24},{24,16},{1,9},{9,1},{17,25},{25,17},{2,10},{10... | collective-permute-start | bytes 399368 | tf_op jit(solution)/shard_map/ppermute | solution.py:640
  21.1 8.2 %collective-permute-start.4 = (bf16[520,128]{1,0:T(8,128)(2,1)S(1)}, bf16[520,128]{1,0:T(8,128)(2,1)S(1)}, u32[]{:S(2)}, u32[]{:S(2)}) collective-permute-start(bf16[520,128]{1,0:T(8,128)(2,1)S(1)} %get-tuple-element.81), channel_id=1, source_target_pairs={{0,16},{8,24},{16,0},{24,8},{1,17},{9,25},{17,1},{25,9},{2,18},{10... | collective-permute-start | bytes 399368 | tf_op jit(solution)/shard_map/ppermute | solution.py:640
  22.6 6.7 %collective-permute-start.5 = (bf16[520,128]{1,0:T(8,128)(2,1)S(1)}, bf16[520,128]{1,0:T(8,128)(2,1)S(1)}, u32[]{:S(2)}, u32[]{:S(2)}) collective-permute-start(bf16[520,128]{1,0:T(8,128)(2,1)S(1)} %get-tuple-element.82), channel_id=1, source_target_pairs={{0,24},{8,16},{16,8},{24,0},{1,25},{9,17},{17,9},{25,1},{2,26},{10... | collective-permute-start | bytes 399368 | tf_op jit(solution)/shard_map/ppermute | solution.py:640
  29.3 36.5 %copy-start.9 = (s32[2]{0:T(128)S(1)}, s32[2]{0:T(128)}, u32[]{:S(2)}) copy-start(s32[2]{0:T(128)} %constant.110) | copy-start | bytes 28
  29.3 36.5 %copy-start.10 = (s32[2]{0:T(128)S(1)}, s32[2]{0:T(128)}, u32[]{:S(2)}) copy-start(s32[2]{0:T(128)} %constant.111) | copy-start | bytes 28
  29.4 9.1 %collective-permute-start.6 = (bf16[136,128]{1,0:T(8,128)(2,1)S(1)}, bf16[136,128]{1,0:T(8,128)(2,1)S(1)}, u32[]{:S(2)}, u32[]{:S(2)}) collective-permute-start(bf16[136,128]{1,0:T(8,128)(2,1)S(1)} %get-tuple-element.88), channel_id=1, source_target_pairs={{0,2},{2,0},{4,6},{6,4},{1,3},{3,1},{5,7},{7,5},{8,10},{10,8},{12,... | collective-permute-start | bytes 104456 | tf_op jit(solution)/shard_map/ppermute | solution.py:640
  33.6 4.9 %collective-permute-start.7 = (bf16[136,128]{1,0:T(8,128)(2,1)S(1)}, bf16[136,128]{1,0:T(8,128)(2,1)S(1)}, u32[]{:S(2)}, u32[]{:S(2)}) collective-permute-start(bf16[136,128]{1,0:T(8,128)(2,1)S(1)} %get-tuple-element.89), channel_id=1, source_target_pairs={{0,4},{2,6},{4,0},{6,2},{1,5},{3,7},{5,1},{7,3},{8,12},{10,14},{12... | collective-permute-start | bytes 104456 | tf_op jit(solution)/shard_map/ppermute | solution.py:640
  33.6 5.7 %collective-permute-start.8 = (bf16[136,128]{1,0:T(8,128)(2,1)S(1)}, bf16[136,128]{1,0:T(8,128)(2,1)S(1)}, u32[]{:S(2)}, u32[]{:S(2)}) collective-permute-start(bf16[136,128]{1,0:T(8,128)(2,1)S(1)} %get-tuple-element.90), channel_id=1, source_target_pairs={{0,6},{2,4},{4,2},{6,0},{1,7},{3,5},{5,3},{7,1},{8,14},{10,12},{12... | collective-permute-start | bytes 104456 | tf_op jit(solution)/shard_map/ppermute | solution.py:640
  40.0 23.1 %all-to-all-start.1 = ((bf16[16,6,32,128]{3,2,1,0:T(8,128)(2,1)}), bf16[16,6,32,128]{3,2,1,0:T(8,128)(2,1)S(1)}, u32[]{:S(2)}, u32[]{:S(2)}) async-start(bf16[16,6,32,128]{3,2,1,0:T(8,128)(2,1)} %constant_dynamic-update-slice_fusion), calls=%async_computation.1 | async-start | bytes 1572864 | tf_op jit(solution)/shard_map/all_to_all | solution.py:854
  46.0 2.2 %collective-permute-start.9 = (s32[1,1]{1,0:T(1,128)}, s32[1,1]{1,0:T(1,128)}, u32[]{:S(2)}, u32[]{:S(2)}) collective-permute-start(s32[1,1]{1,0:T(1,128)} %slice.48), channel_id=1, source_target_pairs={{0,1},{1,0},{2,3},{3,2},{4,5},{5,4},{6,7},{7,6},{8,9},{9,8},{10,11... | collective-permute-start | bytes 20 | tf_op jit(solution)/shard_map/ppermute | solution.py:280

commit v4 on v3

--- a/solution.py
+++ b/solution.py
@@ -11,7 +11,7 @@
 CAP = 25
 PAD = 16
 TABLE = 8
-STEPS = 4
+STEPS = 11
 MIB = 1024 * 1024
 
 

time: 66.2 us -> 66 us (level)
  no operation moved by 1% of the time
where the time goes in v4:
time: 66 us; the launch traced here: 65.6 us
  Pallas kernels  20.4 us (31%)
  waiting for transfers between devices  18.9 us (29%)
  starting transfers between devices  18.8 us (28%)
  between operations  3.98 us (6%)
  local copies, waits for them, and re-layouts  3.45 us (5%)
    all_to_all x1, waiting for transfers between devices, exchange(): return lax.all_to_all(array, axes, split_axis=0, concat_axis=0, tiled=True)  13.6 us
    ppermute x6, starting transfers between devices, swap_all(): got.append(lax.ppermute(parts[step], axis, pairs))  10.2 us
    pallas_call x1, Pallas kernels, convolve_inner(): pl.pallas_call(functools.partial(inner_kernel, tuple(chunks)), out_shape=...  8.68 us
    ppermute x6, waiting for transfers between devices, swap_all(): got.append(lax.ppermute(parts[step], axis, pairs))  5.24 us
    all_to_all x1, starting transfers between devices, exchange(): return lax.all_to_all(array, axes, split_axis=0, concat_axis=0, tiled=True)  4.81 us
    ppermute x2, starting transfers between devices, wire_halo(): got.append(lax.ppermute(rows, 'wire', pairs + [(j, i) for i, j in pairs]))  3.32 us
    pallas_call x1, Pallas kernels, convolve_edges(): pl.pallas_call(functools.partial(edge_kernel, planes), out_shape=(jax.Sha...  2.63 us
    pallas_call x1, Pallas kernels, make_image(): pl.pallas_call(functools.partial(image_kernel, owner_total, share), out_s...  2.61 us
  transfers between devices with their start and end apart: 11, of which 4 were waited for; matrix products, arithmetic and copies ran while one was open for 3% of the time, Pallas kernels for 20%

profile of v4, /device:TPU:0, one launch (start us, length us, event | category | flops | bytes accessed | tf_op | source)
XLA Modules:
  0.0 65.6 jit_solution(14390518868016840959)
XLA Ops:
  0.6 1.9 %prepare.1 = (bf16[256,128]{1,0:T(8,128)(2,1)}, bf16[16,2048]{1,0:T(8,128)(2,1)}, bf16[16,2048]{1,0:T(8,128)(2,1)}, s32[1,128]{1,0:T(1,128)S(1)}, s32[8,128]{1,0:T(8,128)}, /*index=5*/bf16[256,128]{1,0:T(8,128)(2,1)}) custom-call(bf16[256,2048]{1,0:T(8,128)(2,1)} %raw_ref.3, s32[2,128]{1,0:T(2,128)} %bitcast.97, s32[1,102]{1,0:T(1,128)} %bitcast.98, ...), custom_call_target="tpu_custom_call" | custom-call | tf_op jit(solution)/shard_map/prepare/pallas_call | solution.py:156
  3.1 0.7 %copy-done.3 = bf16[1,21,256]{2,1,0:T(8,128)(2,1)S(1)} copy-done((bf16[1,21,256]{2,1,0:T(8,128)(2,1)S(1)}, bf16[1,21,256]{2,1,0:T(8,128)(2,1)}, u32[]{:S(2)}) %copy-start.3) | copy-done | bytes 10776
  3.8 0.6 bands.1.band_ref
  4.7 2.7 %collective-permute-start.1 = (bf16[16,2304]{1,0:T(8,128)(2,1)S(1)}, bf16[16,2304]{1,0:T(8,128)(2,1)S(1)}, u32[]{:S(2)}, u32[]{:S(2)}) collective-permute-start(bf16[16,2304]{1,0:T(8,128)(2,1)S(1)} %get-tuple-element.153), channel_id=1, source_target_pairs={{0,2},{4,6},{2,0},{6,4},{1,3},{5,7},{3,1},{7,5},{8,10},{12,14},{10... | collective-permute-start | bytes 221192 | tf_op jit(solution)/shard_map/ppermute | solution.py:849
  7.4 0.7 collective-permute-start.2
  8.1 8.7 %inner.1.inner_ref = bf16[224,2048]{1,0:T(8,128)(2,1)S(1)} custom-call(bf16[256,2048]{1,0:T(8,128)(2,1)S(1)} %copy-done, bf16[256,128]{1,0:T(8,128)(2,1)S(1)} %copy-done.1, bf16[256,128]{1,0:T(8,128)(2,1)S(1)} %get-tuple-element.159.left_ref, bf16[256,128]{1,0:T(8,128)(2,1)S(1)} %get-tuple-element.158.right_ref, bf16[11,768,256]{2,1,0:T(8,128)(2,1)S(1)} %bands.1.band_ref), custom_call_target="tpu_custom_call" | custom-call | flops 7751073792 | bytes 6291456 | tf_op jit(solution)/shard_map/inner/pallas_call | solution.py:432
  16.9 2.6 %edges.1 = (bf16[256,2048]{1,0:T(8,128)(2,1)S(1)}, bf16[520,128]{1,0:T(8,128)(2,1)S(1)}, bf16[520,128]{1,0:T(8,128)(2,1)S(1)}, bf16[520,128]{1,0:T(8,128)(2,1)S(1)}, bf16[520,128]{1,0:T(8,128)(2,1)S(1)}) custom-call(s32[8,128]{1,0:T(8,128)S(1)} %copy-done.2, s32[1,128]{1,0:T(1,128)S(1)} %get-tuple-element.241.own_ref, bf16[224,2048]{1,0:T(8,128)(2,1)S(1)} %inner.1.inner_ref, ...), custom_call_target="tpu_custom_call" | custom-call | flops 1107296256 | bytes 6291456 | tf_op jit(solution)/shard_map/edges/pallas_call | solution.py:576
  19.5 1.6 %collective-permute-start.3 = (bf16[520,128]{1,0:T(8,128)(2,1)S(1)}, bf16[520,128]{1,0:T(8,128)(2,1)S(1)}, u32[]{:S(2)}, u32[]{:S(2)}) collective-permute-start(bf16[520,128]{1,0:T(8,128)(2,1)S(1)} %get-tuple-element.80), channel_id=1, source_target_pairs={{0,8},{8,0},{16,24},{24,16},{1,9},{9,1},{17,25},{25,17},{2,10},{10... | collective-permute-start | bytes 399368 | tf_op jit(solution)/shard_map/ppermute | solution.py:640
  21.1 1.5 %collective-permute-start.4 = (bf16[520,128]{1,0:T(8,128)(2,1)S(1)}, bf16[520,128]{1,0:T(8,128)(2,1)S(1)}, u32[]{:S(2)}, u32[]{:S(2)}) collective-permute-start(bf16[520,128]{1,0:T(8,128)(2,1)S(1)} %get-tuple-element.81), channel_id=1, source_target_pairs={{0,16},{8,24},{16,0},{24,8},{1,17},{9,25},{17,1},{25,9},{2,18},{10... | collective-permute-start | bytes 399368 | tf_op jit(solution)/shard_map/ppermute | solution.py:640
  23.1 1.8 %pack.1 = bf16[96,32,128]{2,1,0:T(8,128)(2,1)} custom-call(s32[8,128]{1,0:T(8,128)S(1)} %copy-done.2, bf16[256,2048]{1,0:T(8,128)(2,1)S(1)} %get-tuple-element.239.signal_ref), custom_call_target="tpu_custom_call" | custom-call | flops 100000000 | bytes 3145728 | tf_op jit(solution)/shard_map/pack/pallas_call | solution.py:659
  24.9 0.7 %collective-permute-done.3.refs_1_ = bf16[520,128]{1,0:T(8,128)(2,1)S(1)} collective-permute-done((bf16[520,128]{1,0:T(8,128)(2,1)S(1)}, bf16[520,128]{1,0:T(8,128)(2,1)S(1)}, u32[]{:S(2)}, u32[]{:S(2)}) %collective-permute-start.3) | collective-permute-done | bytes 133152 | tf_op jit(solution)/shard_map/ppermute | solution.py:640
  25.6 3.7 %collective-permute-done.4.refs_2_ = bf16[520,128]{1,0:T(8,128)(2,1)S(1)} collective-permute-done((bf16[520,128]{1,0:T(8,128)(2,1)S(1)}, bf16[520,128]{1,0:T(8,128)(2,1)S(1)}, u32[]{:S(2)}, u32[]{:S(2)}) %collective-permute-start.4) | collective-permute-done | bytes 133152 | tf_op jit(solution)/shard_map/ppermute | solution.py:640
  29.4 4.2 %collective-permute-start.6 = (bf16[136,128]{1,0:T(8,128)(2,1)S(1)}, bf16[136,128]{1,0:T(8,128)(2,1)S(1)}, u32[]{:S(2)}, u32[]{:S(2)}) collective-permute-start(bf16[136,128]{1,0:T(8,128)(2,1)S(1)} %get-tuple-element.88), channel_id=1, source_target_pairs={{0,2},{2,0},{4,6},{6,4},{1,3},{3,1},{5,7},{7,5},{8,10},{10,8},{12,... | collective-permute-start | bytes 104456 | tf_op jit(solution)/shard_map/ppermute | solution.py:640
  33.6 2.4 %collective-permute-start.8 = (bf16[136,128]{1,0:T(8,128)(2,1)S(1)}, bf16[136,128]{1,0:T(8,128)(2,1)S(1)}, u32[]{:S(2)}, u32[]{:S(2)}) collective-permute-start(bf16[136,128]{1,0:T(8,128)(2,1)S(1)} %get-tuple-element.90), channel_id=1, source_target_pairs={{0,6},{2,4},{4,2},{6,0},{1,7},{3,5},{5,3},{7,1},{8,14},{10,12},{12... | collective-permute-start | bytes 104456 | tf_op jit(solution)/shard_map/ppermute | solution.py:640
  36.0 0.6 slice.47
  38.5 0.8 %collective-permute-done.8.refs_3_ = bf16[136,128]{1,0:T(8,128)(2,1)S(1)} collective-permute-done((bf16[136,128]{1,0:T(8,128)(2,1)S(1)}, bf16[136,128]{1,0:T(8,128)(2,1)S(1)}, u32[]{:S(2)}, u32[]{:S(2)}) %collective-permute-start.8) | collective-permute-done | bytes 34848 | tf_op jit(solution)/shard_map/ppermute | solution.py:640
  39.3 0.6 constant_dynamic-update-slice_fusion
  39.9 4.8 %all-to-all-start.1 = ((bf16[16,6,32,128]{3,2,1,0:T(8,128)(2,1)}), bf16[16,6,32,128]{3,2,1,0:T(8,128)(2,1)S(1)}, u32[]{:S(2)}, u32[]{:S(2)}) async-start(bf16[16,6,32,128]{3,2,1,0:T(8,128)(2,1)} %constant_dynamic-update-slice_fusion), calls=%async_computation.1 | async-start | bytes 1572864 | tf_op jit(solution)/shard_map/all_to_all | solution.py:854
  44.8 0.6 receive_plan.1
  45.3 0.6 slice.48
  46.0 0.7 %copy.29 = s32[16,128]{0,1:T(8,128)} copy(s32[16,128]{1,0:T(8,128)S(1)} %get-tuple-element.123) | data formatting | bytes 16384 | tf_op jit(solution)/shard_map/while | solution.py:901
  46.7 1.4 %stage.1.staged_ref = bf16[26,128,256]{2,1,0:T(8,128)(2,1)S(1)} custom-call(s32[8,128]{1,0:T(8,128)S(1)} %get-tuple-element.242.plan_ref, bf16[128,32,128]{2,1,0:T(8,128)(2,1)S(1)} %copy-done.4), custom_call_target="tpu_custom_call" | custom-call | flops 100000000 | bytes 3145728 | tf_op jit(solution)/shard_map/stage/pallas_call | solution.py:683
  49.4 13.6 %all-to-all-done.1 = bf16[16,6,32,128]{3,2,1,0:T(8,128)(2,1)S(1)} async-done(((bf16[16,6,32,128]{3,2,1,0:T(8,128)(2,1)}), bf16[16,6,32,128]{3,2,1,0:T(8,128)(2,1)S(1)}, u32[]{:S(2)}, u32[]{:S(2)}) %all-to-all-start.1) | async-done | bytes 786464 | tf_op jit(solution)/shard_map/all_to_all | solution.py:854
  63.0 2.6 %image.1 = f32[128,2048]{1,0:T(8,128)} custom-call(s32[8,128]{1,0:T(8,128)S(1)} %get-tuple-element.242.plan_ref, bf16[96,32,128]{2,1,0:T(8,128)(2,1)S(1)} %bitcast.89, bf16[26,128,256]{2,1,0:T(8,128)(2,1)S(1)} %stage.1.staged_ref), custom_call_target="tpu_custom_call" | custom-call | flops 100000000 | bytes 3145728 | tf_op jit(solution)/shard_map/image/pallas_call | solution.py:732
  (37 shorter events, 1.4 us)
Async XLA Ops:
  0.6 7.4 %copy-start = (bf16[256,2048]{1,0:T(8,128)(2,1)S(1)}, bf16[256,2048]{1,0:T(8,128)(2,1)}, u32[]{:S(2)}) copy-start(bf16[256,2048]{1,0:T(8,128)(2,1)} %raw_ref.3) | copy-start | bytes 3145732
  2.6 5.5 %copy-start.1 = (bf16[256,128]{1,0:T(8,128)(2,1)S(1)}, bf16[256,128]{1,0:T(8,128)(2,1)}, u32[]{:S(2)}) copy-start(bf16[256,128]{1,0:T(8,128)(2,1)} %get-tuple-element.74.mask_ref) | copy-start | bytes 196612
  2.6 1.9 %collective-permute-start = (bf16[256,128]{1,0:T(8,128)(2,1)}, bf16[256,128]{1,0:T(8,128)(2,1)S(1)}, u32[]{:S(2)}, u32[]{:S(2)}) collective-permute-start(bf16[256,128]{1,0:T(8,128)(2,1)} %get-tuple-element.75), channel_id=1, source_target_pairs={{0,1},{1,0},{2,3},{3,2},{4,5},{5,4},{6,7},{7,6},{8,9},{9,8},{10,11... | collective-permute-start | bytes 196616 | tf_op jit(solution)/shard_map/ppermute | solution.py:833
  3.1 0.7 %copy-start.3 = (bf16[1,21,256]{2,1,0:T(8,128)(2,1)S(1)}, bf16[1,21,256]{2,1,0:T(8,128)(2,1)}, u32[]{:S(2)}) copy-start(bf16[1,21,256]{2,1,0:T(8,128)(2,1)} %param.10) | copy-start | bytes 32260
  3.8 0.8 %copy-start.7 = (bf16[16,2048]{1,0:T(8,128)(2,1)S(1)}, bf16[16,2048]{1,0:T(8,128)(2,1)}, u32[]{:S(2)}) copy-start(bf16[16,2048]{1,0:T(8,128)(2,1)} %get-tuple-element.76) | copy-start | bytes 196612
  3.8 0.9 %copy-start.8 = (bf16[16,2048]{1,0:T(8,128)(2,1)S(1)}, bf16[16,2048]{1,0:T(8,128)(2,1)}, u32[]{:S(2)}) copy-start(bf16[16,2048]{1,0:T(8,128)(2,1)} %get-tuple-element.77) | copy-start | bytes 196612
  4.7 12.1 %collective-permute-start.1 = (bf16[16,2304]{1,0:T(8,128)(2,1)S(1)}, bf16[16,2304]{1,0:T(8,128)(2,1)S(1)}, u32[]{:S(2)}, u32[]{:S(2)}) collective-permute-start(bf16[16,2304]{1,0:T(8,128)(2,1)S(1)} %get-tuple-element.153), channel_id=1, source_target_pairs={{0,2},{4,6},{2,0},{6,4},{1,3},{5,7},{3,1},{7,5},{8,10},{12,14},{10... | collective-permute-start | bytes 221192 | tf_op jit(solution)/shard_map/ppermute | solution.py:849
  7.4 9.4 %collective-permute-start.2 = (bf16[16,2304]{1,0:T(8,128)(2,1)S(1)}, bf16[16,2304]{1,0:T(8,128)(2,1)S(1)}, u32[]{:S(2)}, u32[]{:S(2)}) collective-permute-start(bf16[16,2304]{1,0:T(8,128)(2,1)S(1)} %get-tuple-element.152), channel_id=1, source_target_pairs={{2,4},{4,2},{3,5},{5,3},{10,12},{12,10},{11,13},{13,11},{18,20},{2... | collective-permute-start | bytes 221192 | tf_op jit(solution)/shard_map/ppermute | solution.py:849
  8.1 8.8 %copy-start.2 = (s32[8,128]{1,0:T(8,128)S(1)}, s32[8,128]{1,0:T(8,128)}, u32[]{:S(2)}) copy-start(s32[8,128]{1,0:T(8,128)} %get-tuple-element.72.plan_ref) | copy-start | bytes 12292
  8.1 8.8 %copy-start.4 = (bf16[128,32,128]{2,1,0:T(8,128)(2,1)S(1)}, bf16[128,32,128]{2,1,0:T(8,128)(2,1)}, u32[]{:S(2)}) copy-start(bf16[128,32,128]{2,1,0:T(8,128)(2,1)} %geo_ref.3) | copy-start | bytes 3145732
  19.5 20.5 %copy-start.5 = (bf16[256,2048]{1,0:T(8,128)(2,1)}, bf16[256,2048]{1,0:T(8,128)(2,1)S(1)}, u32[]{:S(2)}) copy-start(bf16[256,2048]{1,0:T(8,128)(2,1)S(1)} %get-tuple-element.239.signal_ref) | copy-start | bytes 3145732
  19.5 6.1 %collective-permute-start.3 = (bf16[520,128]{1,0:T(8,128)(2,1)S(1)}, bf16[520,128]{1,0:T(8,128)(2,1)S(1)}, u32[]{:S(2)}, u32[]{:S(2)}) collective-permute-start(bf16[520,128]{1,0:T(8,128)(2,1)S(1)} %get-tuple-element.80), channel_id=1, source_target_pairs={{0,8},{8,0},{16,24},{24,16},{1,9},{9,1},{17,25},{25,17},{2,10},{10... | collective-permute-start | bytes 399368 | tf_op jit(solution)/shard_map/ppermute | solution.py:640
  21.1 8.2 %collective-permute-start.4 = (bf16[520,128]{1,0:T(8,128)(2,1)S(1)}, bf16[520,128]{1,0:T(8,128)(2,1)S(1)}, u32[]{:S(2)}, u32[]{:S(2)}) collective-permute-start(bf16[520,128]{1,0:T(8,128)(2,1)S(1)} %get-tuple-element.81), channel_id=1, source_target_pairs={{0,16},{8,24},{16,0},{24,8},{1,17},{9,25},{17,1},{25,9},{2,18},{10... | collective-permute-start | bytes 399368 | tf_op jit(solution)/shard_map/ppermute | solution.py:640
  22.6 6.7 %collective-permute-start.5 = (bf16[520,128]{1,0:T(8,128)(2,1)S(1)}, bf16[520,128]{1,0:T(8,128)(2,1)S(1)}, u32[]{:S(2)}, u32[]{:S(2)}) collective-permute-start(bf16[520,128]{1,0:T(8,128)(2,1)S(1)} %get-tuple-element.82), channel_id=1, source_target_pairs={{0,24},{8,16},{16,8},{24,0},{1,25},{9,17},{17,9},{25,1},{2,26},{10... | collective-permute-start | bytes 399368 | tf_op jit(solution)/shard_map/ppermute | solution.py:640
  29.3 36.3 %copy-start.9 = (s32[2]{0:T(128)S(1)}, s32[2]{0:T(128)}, u32[]{:S(2)}) copy-start(s32[2]{0:T(128)} %constant.110) | copy-start | bytes 28
  29.3 36.3 %copy-start.10 = (s32[2]{0:T(128)S(1)}, s32[2]{0:T(128)}, u32[]{:S(2)}) copy-start(s32[2]{0:T(128)} %constant.111) | copy-start | bytes 28
  29.4 9.1 %collective-permute-start.6 = (bf16[136,128]{1,0:T(8,128)(2,1)S(1)}, bf16[136,128]{1,0:T(8,128)(2,1)S(1)}, u32[]{:S(2)}, u32[]{:S(2)}) collective-permute-start(bf16[136,128]{1,0:T(8,128)(2,1)S(1)} %get-tuple-element.88), channel_id=1, source_target_pairs={{0,2},{2,0},{4,6},{6,4},{1,3},{3,1},{5,7},{7,5},{8,10},{10,8},{12,... | collective-permute-start | bytes 104456 | tf_op jit(solution)/shard_map/ppermute | solution.py:640
  33.6 4.9 %collective-permute-start.7 = (bf16[136,128]{1,0:T(8,128)(2,1)S(1)}, bf16[136,128]{1,0:T(8,128)(2,1)S(1)}, u32[]{:S(2)}, u32[]{:S(2)}) collective-permute-start(bf16[136,128]{1,0:T(8,128)(2,1)S(1)} %get-tuple-element.89), channel_id=1, source_target_pairs={{0,4},{2,6},{4,0},{6,2},{1,5},{3,7},{5,1},{7,3},{8,12},{10,14},{12... | collective-permute-start | bytes 104456 | tf_op jit(solution)/shard_map/ppermute | solution.py:640
  33.6 5.7 %collective-permute-start.8 = (bf16[136,128]{1,0:T(8,128)(2,1)S(1)}, bf16[136,128]{1,0:T(8,128)(2,1)S(1)}, u32[]{:S(2)}, u32[]{:S(2)}) collective-permute-start(bf16[136,128]{1,0:T(8,128)(2,1)S(1)} %get-tuple-element.90), channel_id=1, source_target_pairs={{0,6},{2,4},{4,2},{6,0},{1,7},{3,5},{5,3},{7,1},{8,14},{10,12},{12... | collective-permute-start | bytes 104456 | tf_op jit(solution)/shard_map/ppermute | solution.py:640
  39.9 23.1 %all-to-all-start.1 = ((bf16[16,6,32,128]{3,2,1,0:T(8,128)(2,1)}), bf16[16,6,32,128]{3,2,1,0:T(8,128)(2,1)S(1)}, u32[]{:S(2)}, u32[]{:S(2)}) async-start(bf16[16,6,32,128]{3,2,1,0:T(8,128)(2,1)} %constant_dynamic-update-slice_fusion), calls=%async_computation.1 | async-start | bytes 1572864 | tf_op jit(solution)/shard_map/all_to_all | solution.py:854
  45.9 2.2 %collective-permute-start.9 = (s32[1,1]{1,0:T(1,128)}, s32[1,1]{1,0:T(1,128)}, u32[]{:S(2)}, u32[]{:S(2)}) collective-permute-start(s32[1,1]{1,0:T(1,128)} %slice.48), channel_id=1, source_target_pairs={{0,1},{1,0},{2,3},{3,2},{4,5},{5,4},{6,7},{7,6},{8,9},{9,8},{10,11... | collective-permute-start | bytes 20 | tf_op jit(solution)/shard_map/ppermute | solution.py:280
